TPU v7x, 1024 devices: a whole 4x8x16 slice. The times are simulated.
1024 devices in a mesh: gx: 8 (over x, y_lo), gy: 8 (over y_hi, core), gz: 16 (over z).
Axes of the slice: x: 4, y: 8 (y_hi: 4, y_lo: 2; y = y_hi * 2 + y_lo), z: 16, core: 2. Of those that a mesh axis runs over, the one named last changes fastest.
Arguments:
- spectrum: float32 [3, 2, 64, 64, 2048], P(None, None, ('gy', 'gx'), None, 'gz'), may hold values from -0.3125 to 0.3125
- theta: float32 [64, 64, 8192], P('gy', 'gz', 'gx'), may hold values from -6 to 6
- section_sum: float32 [64, 64, 8192], P('gy', 'gz', 'gx'), may hold values from -6 to 6
- seg_offset: int32 [8], replicated, may hold values from 0 to 3328, as said below
- seg_length: int32 [8], replicated, may hold values from 256 to 768, as said below
- stencil_index: int32 [8, 8192], replicated, may hold values from 0 to 767, as said below
- stencil_weight: float32 [8, 8192], replicated, may hold values from 0 to 0.25
Outputs:
- theta_next: float32 [64, 64, 8192], P('gy', 'gz', 'gx')
- section_next: float32 [64, 64, 8192], P('gy', 'gz', 'gx')
Inputs may be any that keep to these rules, and one draw needn't show every extreme that they name: `seg_length`: some block's segment holds exactly 768 cells. For every block i, seg_offset[i] + 768 <= 4096. `stencil_index`: positions count from the start of the segment of the scalar cell's x block; taps at or past that segment's length are padding.
All inputs are finite; a program needn't handle non-finite values.
Results may differ from a plain program's by a relative error of at most 0.00005.
Values sent between devices are 32-bit elements; how exact they have to be, the bound alone decides.
No kernel may reach another device: no remote copies, remote signals or barrier semaphores. Data moves between devices by JAX's collectives and lax.ppermute only.
A program may use at most 64 MiB of HBM per device.

v0:
```python
import math

import jax
import jax.numpy as jnp
from jax import lax
from jax.sharding import PartitionSpec as P

first_coeffs = (0.8, -0.2, 4.0 / 105.0, -1.0 / 280.0)
second_coeffs = (1.6, -0.2, 8.0 / 315.0, -1.0 / 560.0)
center_coeff = -205.0 / 72.0
diffusivity = 0.15
time_step = 0.4
section_keep = -5.0 / 9.0
section_gain = 15.0 / 16.0


def padded_2(shard, sides, width):
    edges = {}
    for axis, dim in sides:
        count, length = (lax.axis_size(axis), shard.shape[dim])
        up = [(i, (i + 1) % count) for i in range(count)]
        last = lax.slice_in_dim(shard, length - width, length, axis=dim)
        leading = lax.slice_in_dim(shard, 0, width, axis=dim)
        edges[dim] = (
            lax.ppermute(last, axis, up),
            lax.ppermute(leading, axis, [(b, a) for a, b in up]),
        )
    done = []
    for _, dim in sides:
        low, high = edges[dim]
        around = [(width, width) if d in done else (0, 0) for d in range(shard.ndim)]
        shard = jnp.concatenate([jnp.pad(low, around), shard, jnp.pad(high, around)], axis=dim)
        done.append(dim)
    return shard


def contract(pattern, first_term, second_term):
    return jnp.einsum(pattern, first_term, second_term, precision=lax.Precision.HIGHEST)


def phase_table(rows_index, cols_index, period):
    wound = rows_index[:, None] * cols_index[None, :] % period
    angle = 2.0 * math.pi / period * wound.astype(jnp.float32)
    return (jnp.cos(angle), jnp.sin(angle))


def inverse_lines(spectrum):
    mode_count = spectrum.shape[-1]
    length = 2 * mode_count
    factor = math.isqrt(length)
    line_shape = (3,) + spectrum.shape[2:4] + (factor // 2, factor)
    real_part = spectrum[:, 0].reshape(line_shape)
    imag_part = spectrum[:, 1].reshape(line_shape)
    outer_index = jnp.arange(factor // 2, dtype=jnp.int32)
    inner_index = jnp.arange(factor, dtype=jnp.int32)
    cosine_first, sine_first = phase_table(outer_index, inner_index, factor)
    first_real = contract("cyzak,aj->cyzjk", real_part, cosine_first) - contract(
        "cyzak,aj->cyzjk", imag_part, sine_first
    )
    first_imag = contract("cyzak,aj->cyzjk", real_part, sine_first) + contract(
        "cyzak,aj->cyzjk", imag_part, cosine_first
    )
    cosine_twist, sine_twist = phase_table(inner_index, inner_index, length)
    twist_real = first_real * cosine_twist - first_imag * sine_twist
    twist_imag = first_real * sine_twist + first_imag * cosine_twist
    cosine_last, sine_last = phase_table(inner_index, inner_index, factor)
    physical = contract("cyzjk,km->cyzmj", twist_real, cosine_last) - contract(
        "cyzjk,km->cyzmj", twist_imag, sine_last
    )
    return physical.reshape((3,) + spectrum.shape[2:4] + (length,))


def pick_entry(table, entry):
    return jnp.sum(jnp.where(jnp.arange(table.shape[0], dtype=jnp.int32) == entry, table, 0))


def interpolate(segment, taps_index, taps_weight, live_count):
    live_weight = jnp.where(taps_index < live_count, taps_weight, 0.0)
    position = jnp.arange(segment.shape[-1], dtype=jnp.int32)
    matrix = jnp.zeros((segment.shape[-1], taps_index.shape[1]), jnp.float32)
    for tap_number in range(taps_index.shape[0]):
        matrix = matrix + jnp.where(
            position[:, None] == taps_index[tap_number][None, :],
            live_weight[tap_number][None, :],
            0.0,
        )
    return contract("cyzm,ms->cyzs", segment, matrix)


def body(spectrum, theta, section_sum, seg_offset, seg_length, stencil_index, stencil_weight):
    blocks = lax.axis_size("gx")
    columns = lax.all_to_all(spectrum, "gz", split_axis=3, concat_axis=4, tiled=True)
    velocity = inverse_lines(columns)
    line_length = velocity.shape[-1]
    widest = 3 * line_length // (2 * blocks)
    block_cells = stencil_index.shape[1] // blocks
    block_numbers = jnp.arange(blocks, dtype=jnp.int32)

    def cut_block(block_number):
        return lax.dynamic_slice_in_dim(velocity, pick_entry(seg_offset, block_number), widest, 3)

    pieces = lax.map(cut_block, block_numbers)
    arrived = lax.all_to_all(pieces, "gx", split_axis=0, concat_axis=2, tiled=True)[0]
    block_number = lax.axis_index("gx")
    taps_index = lax.dynamic_slice_in_dim(stencil_index, block_number * block_cells, block_cells, 1)
    taps_weight = lax.dynamic_slice_in_dim(
        stencil_weight, block_number * block_cells, block_cells, 1
    )
    taps_index, taps_weight, seg_start, live_count = (
        taps_index,
        taps_weight,
        pick_entry(seg_offset, block_number),
        pick_entry(seg_length, block_number),
    )
    carried = interpolate(arrived, taps_index, taps_weight, live_count)
    padded = padded_2(theta, (("gx", 2), ("gy", 0), ("gz", 1)), 4)
    rows_count, depth, cells = theta.shape

    def window(along_y, along_z, along_x):
        return padded[
            4 + along_y : 4 + along_y + rows_count,
            4 + along_z : 4 + along_z + depth,
            4 + along_x : 4 + along_x + cells,
        ]

    grad_x = jnp.zeros_like(theta)
    grad_y = jnp.zeros_like(theta)
    grad_z = jnp.zeros_like(theta)
    laplace = 3.0 * center_coeff * theta
    for reach in range(1, 5):
        ahead_x = window(0, 0, reach)
        behind_x = window(0, 0, -reach)
        ahead_y = window(reach, 0, 0)
        behind_y = window(-reach, 0, 0)
        ahead_z = window(0, reach, 0)
        behind_z = window(0, -reach, 0)
        first = first_coeffs[reach - 1]
        second = second_coeffs[reach - 1]
        grad_x = grad_x + first * (ahead_x - behind_x)
        grad_y = grad_y + first * (ahead_y - behind_y)
        grad_z = grad_z + first * (ahead_z - behind_z)
        laplace = laplace + second * (ahead_x + behind_x + ahead_y + behind_y + ahead_z + behind_z)
    change = (
        -(carried[0] * grad_x + carried[1] * grad_y + carried[2] * grad_z) + diffusivity * laplace
    )
    section_next = section_keep * section_sum + time_step * change
    theta_next = theta + section_gain * section_next
    return (theta_next, section_next)


def solution(mesh):
    placed = (
        P(None, None, ("gy", "gx"), None, "gz"),
        P("gy", "gz", "gx"),
        P("gy", "gz", "gx"),
        P(),
        P(),
        P(),
        P(),
    )
    return jax.shard_map(
        body,
        mesh=mesh,
        in_specs=placed,
        out_specs=(P("gy", "gz", "gx"), P("gy", "gz", "gx")),
        check_vma=False,
    )
```

profile of v0, /device:TPU:1, one launch (start us, length us, event | category | flops | bytes accessed | tf_op | source)
XLA Modules:
  0.0 110.3 jit_solution(4732723401181167860)
XLA Ops:
  0.6 1.0 constant_dynamic-update-slice_fusion.1
  1.6 4.8 %collective-permute-start.5 = (f32[8,4,1024]{2,0,1:T(8,128)S(1)}, f32[8,4,1024]{2,0,1:T(8,128)S(1)}, u32[]{:S(2)}, u32[]{:S(2)}) collective-permute-start(f32[8,4,1024]{2,0,1:T(8,128)S(1)} %get-tuple-element.61), channel_id=1, source_target_pairs={{0,1},{1,2},{2,3},{3,4},{4,5},{5,6},{6,7},{7,8},{8,9},{9,10},{10,1... | collective-permute-start | bytes 393224 | tf_op jit(solution)/shard_map/ppermute | solution.py:25
  6.5 15.9 %collective-permute-start.4 = (f32[8,4,1024]{2,0,1:T(8,128)S(1)}, f32[8,4,1024]{2,0,1:T(8,128)S(1)}, u32[]{:S(2)}, u32[]{:S(2)}) collective-permute-start(f32[8,4,1024]{2,0,1:T(8,128)S(1)} %get-tuple-element.61), channel_id=1, source_target_pairs={{1,0},{2,1},{3,2},{4,3},{5,4},{6,5},{7,6},{8,7},{9,8},{10,9},{11,1... | collective-permute-start | bytes 393224 | tf_op jit(solution)/shard_map/ppermute | solution.py:26
  22.3 1.8 %copy.48 = f32[3,2,1,64,128]{4,0,2,1,3:T(4,128)} copy(f32[3,2,1,64,128]{4,3,2,1,0:T(8,128)} %param.9) | data formatting | bytes 393216 | tf_op args[0]
  24.1 5.3 %all-to-all-start = ((f32[3,2,1,64,128]{4,0,2,1,3:T(4,128)}), f32[3,2,1,64,128]{4,0,2,1,3:T(4,128)S(1)}, u32[]{:S(2)}, u32[]{:S(2)}) async-start(f32[3,2,1,64,128]{4,0,2,1,3:T(4,128)} %copy.48), calls=%async_computation | async-start | bytes 524288 | tf_op jit(solution)/shard_map/all_to_all | solution.py:92
  29.5 5.4 %collective-permute-start = (f32[8,4,4]{2,0,1:T(8,128)S(1)}, f32[8,4,4]{2,0,1:T(8,128)S(1)}, u32[]{:S(2)}, u32[]{:S(2)}) collective-permute-start(f32[8,4,4]{2,0,1:T(8,128)S(1)} %get-tuple-element.64), channel_id=1, source_target_pairs={{128,0},{256,128},{384,256},{512,384},{640,512},{768,640},{896,768... | collective-permute-start | bytes 1544 | tf_op jit(solution)/shard_map/ppermute | solution.py:26
  34.9 1.9 %collective-permute-start.1 = (f32[8,4,4]{2,0,1:T(8,128)S(1)}, f32[8,4,4]{2,0,1:T(8,128)S(1)}, u32[]{:S(2)}, u32[]{:S(2)}) collective-permute-start(f32[8,4,4]{2,0,1:T(8,128)S(1)} %get-tuple-element.65), channel_id=1, source_target_pairs={{0,128},{128,256},{256,384},{384,512},{512,640},{640,768},{768,896... | collective-permute-start | bytes 1544 | tf_op jit(solution)/shard_map/ppermute | solution.py:25
  36.8 5.9 %collective-permute-start.3 = (f32[4,4,1024]{2,0,1:T(4,128)S(1)}, f32[4,4,1024]{2,0,1:T(4,128)S(1)}, u32[]{:S(2)}, u32[]{:S(2)}) collective-permute-start(f32[4,4,1024]{2,0,1:T(4,128)S(1)} %get-tuple-element.62), channel_id=1, source_target_pairs={{0,16},{16,32},{32,48},{48,64},{64,80},{80,96},{96,112},{112,0},{1... | collective-permute-start | bytes 196616 | tf_op jit(solution)/shard_map/ppermute | solution.py:25
  43.9 1.4 %dynamic-slice_select_fusion = f32[8,1024]{1,0:T(8,128)S(1)} fusion(f32[8,8192]{1,0:T(8,128)} %param.15, s32[]{:T(128)S(6)} %select_n.84, s32[8,8192]{1,0:T(8,128)} %param.14, s32[]{:T(128)} %fusion.114), kind=kLoop, calls=%fused_computation.125 | loop fusion | flops 16384 | bytes 98312 | tf_op jit(solution)/shard_map/jit(_where)/select_n | solution.py:78
  48.3 1.3 %fusion.39 = f32[64,3,4,64]{3,0,2,1:T(8,128)S(1)} fusion(f32[64,3,1,4,64]{4,0,3,1,2:T(8,128)S(1)} %fusion.36, f32[64,3,1,4,64]{4,0,3,1,2:T(8,128)S(1)} %fusion.37, f32[64,64]{1,0:T(8,128)S(1)} %copy.51, f32[64,64]{1,0:T(8,128)S(1)} %copy.50), kind=kOutput, calls=%fused_computation.68 | convolution fusion | flops 37953536 | bytes 622592 | tf_op jit(solution)/shard_map/cyzjk,km->cyzmj/dot_general | solution.py:38
  49.6 1.4 %fusion.35 = f32[3,1,4,64,64]{4,3,2,0,1:T(8,128)S(1)} fusion(f32[64,3,4,64]{3,0,2,1:T(8,128)S(1)} %fusion.39, f32[64,3,1,4,64]{4,0,3,1,2:T(8,128)S(1)} %fusion.36, f32[64,3,1,4,64]{4,0,3,1,2:T(8,128)S(1)} %fusion.37, f32[64,64]{1,0:T(8,128)S(1)} %copy.51, f32[64,64]{1,0:T(8,128)S(1)} %copy.50), kind=kOutput, calls=%fused_computation.46 | convolution fusion | flops 38002688 | bytes 819200 | tf_op jit(solution)/shard_map/cyzjk,km->cyzmj/dot_general | solution.py:38
  51.6 33.9 %while.10 = (s32[]{:T(128)}, f32[8,3,1,4,768]{4,3,2,1,0:T(4,128)}, s32[8]{0:T(128)S(1)}, s32[8]{0:T(128)S(1)}, f32[3,1,4,4096]{3,2,0,1:T(4,128)S(1)}, /*index=5*/s32[]{:T(128)}, s32[]{:T(128)}, s32[]{:T(128)}) while((s32[]{:T(128)}, f32[8,3,1,4,768]{4,3,2,1,0:T(4,128)}, s32[8]{0:T(128)S(1)}, s32[8]{0:T(128)S(1)}, ...), condition=%wide.region_2.3_spmd, body=%wide.region_0.2_spmd.sunk | while | flops 28 | bytes 73915 | solution.py:102
  52.2 1.3 %fusion.144 = s32[]{:T(128)} fusion(s32[8]{0:T(128)S(1)} %get-tuple-element.124, s32[]{:T(128)} %bitcast.127), kind=kLoop, calls=%fused_computation.2.clone.1 | loop fusion | flops 23 | bytes 40 | tf_op jit(solution)/shard_map/while/body/eval_jaxpr/reduce_sum | solution.py:74
  55.1 0.7 bitcast_dynamic-update-slice_fusion.2
  56.4 1.3 %fusion.144 = s32[]{:T(128)} fusion(s32[8]{0:T(128)S(1)} %get-tuple-element.124, s32[]{:T(128)} %bitcast.127), kind=kLoop, calls=%fused_computation.2.clone.1 | loop fusion | flops 23 | bytes 40 | tf_op jit(solution)/shard_map/while/body/eval_jaxpr/reduce_sum | solution.py:74
  60.7 1.3 %fusion.144 = s32[]{:T(128)} fusion(s32[8]{0:T(128)S(1)} %get-tuple-element.124, s32[]{:T(128)} %bitcast.127), kind=kLoop, calls=%fused_computation.2.clone.1 | loop fusion | flops 23 | bytes 40 | tf_op jit(solution)/shard_map/while/body/eval_jaxpr/reduce_sum | solution.py:74
  64.9 1.3 %fusion.144 = s32[]{:T(128)} fusion(s32[8]{0:T(128)S(1)} %get-tuple-element.124, s32[]{:T(128)} %bitcast.127), kind=kLoop, calls=%fused_computation.2.clone.1 | loop fusion | flops 23 | bytes 40 | tf_op jit(solution)/shard_map/while/body/eval_jaxpr/reduce_sum | solution.py:74
  67.9 0.7 bitcast_dynamic-update-slice_fusion.2
  69.2 1.3 %fusion.144 = s32[]{:T(128)} fusion(s32[8]{0:T(128)S(1)} %get-tuple-element.124, s32[]{:T(128)} %bitcast.127), kind=kLoop, calls=%fused_computation.2.clone.1 | loop fusion | flops 23 | bytes 40 | tf_op jit(solution)/shard_map/while/body/eval_jaxpr/reduce_sum | solution.py:74
  72.1 0.7 bitcast_dynamic-update-slice_fusion.2
  73.4 1.3 %fusion.144 = s32[]{:T(128)} fusion(s32[8]{0:T(128)S(1)} %get-tuple-element.124, s32[]{:T(128)} %bitcast.127), kind=kLoop, calls=%fused_computation.2.clone.1 | loop fusion | flops 23 | bytes 40 | tf_op jit(solution)/shard_map/while/body/eval_jaxpr/reduce_sum | solution.py:74
  77.6 1.3 %fusion.144 = s32[]{:T(128)} fusion(s32[8]{0:T(128)S(1)} %get-tuple-element.124, s32[]{:T(128)} %bitcast.127), kind=kLoop, calls=%fused_computation.2.clone.1 | loop fusion | flops 23 | bytes 40 | tf_op jit(solution)/shard_map/while/body/eval_jaxpr/reduce_sum | solution.py:74
  81.9 1.3 %fusion.144 = s32[]{:T(128)} fusion(s32[8]{0:T(128)S(1)} %get-tuple-element.124, s32[]{:T(128)} %bitcast.127), kind=kLoop, calls=%fused_computation.2.clone.1 | loop fusion | flops 23 | bytes 40 | tf_op jit(solution)/shard_map/while/body/eval_jaxpr/reduce_sum | solution.py:74
  84.8 0.7 bitcast_dynamic-update-slice_fusion.2
  85.5 5.1 %all-to-all-start.1 = ((f32[8,3,1,4,768]{4,3,1,2,0:T(4,128)}), f32[8,3,1,4,768]{4,3,1,2,0:T(4,128)S(1)}, u32[]{:S(2)}, u32[]{:S(2)}) async-start(f32[8,3,1,4,768]{4,3,1,2,0:T(4,128)} %bitcast.22), calls=%async_computation.1 | async-start | bytes 589824 | tf_op jit(solution)/shard_map/all_to_all | solution.py:103
  90.7 1.2 %constant_dynamic-slice_fusion = (s32[1,1024]{1,0:T(1,128)S(1)}, s32[1,1024]{1,0:T(1,128)S(1)}, s32[1,1024]{1,0:T(1,128)S(1)}, s32[1,1024]{1,0:T(1,128)S(1)}, s3...) fusion(s32[8,8192]{1,0:T(8,128)} %param.14, s32[]{:T(128)S(6)} %select_n.84, ...), kind=kLoop, calls=%fused_computation.164 | loop fusion | bytes 65568 | tf_op jit(solution)/shard_map/slice | solution.py:83
  91.9 6.2 %collective-permute-start.2 = (f32[4,4,1024]{2,0,1:T(4,128)S(1)}, f32[4,4,1024]{2,0,1:T(4,128)S(1)}, u32[]{:S(2)}, u32[]{:S(2)}) collective-permute-start(f32[4,4,1024]{2,0,1:T(4,128)S(1)} %get-tuple-element.63), channel_id=1, source_target_pairs={{16,0},{32,16},{48,32},{64,48},{80,64},{96,80},{112,96},{0,112},{1... | collective-permute-start | bytes 196616 | tf_op jit(solution)/shard_map/ppermute | solution.py:26
  98.3 3.8 %collective-permute-done.2 = f32[4,4,1024]{2,0,1:T(4,128)S(1)} collective-permute-done((f32[4,4,1024]{2,0,1:T(4,128)S(1)}, f32[4,4,1024]{2,0,1:T(4,128)S(1)}, u32[]{:S(2)}, u32[]{:S(2)}) %collective-permute-start.2) | collective-permute-done | bytes 65568 | tf_op jit(solution)/shard_map/ppermute | solution.py:26
  102.5 5.1 %fusion.1 = f32[3,8,4,1024]{3,1,2,0:T(8,128)S(1)} fusion(f32[1024]{0:T(1024)S(1)} %bitcast.130, s32[1024]{0:T(1024)S(1)} %bitcast.138, f32[1024]{0:T(1024)S(1)} %bitcast.131, s32[1024]{0:T(1024)S(1)} %bitcast.139, f32[1024]{0:T(1024)S(1)} %bitcast.132, s32[1024]{0:T(1024)S(1)} %bitcast.140, f32[1024]{0:T(1024)S(1)} %bitcast.133, s32[1024]{0:T(1024)S(1)} %bitcast.141, ...), kind=kOutput, calls=%fused_computation.3 | convolution fusion | flops 924057600 | bytes 753664 | tf_op jit(solution)/shard_map/cyzm,ms->cyzs/dot_general | solution.py:38
  107.6 1.2 %multiply_add_fusion = (f32[8,4,1024]{2,0,1:T(8,128)S(1)}, f32[8,4,1024]{2,0,1:T(8,128)S(1)}) fusion(f32[8,4,1024]{2,1,0:T(4,128)S(1)} %copy-done, f32[8,4,1024]{2,0,1:T(8,128)S(1)} %collective-permute-done.5, f32[8,4,1024]{2,0,1:T(8,128)S(1)} %collective-permute-done.4, f32[8,4,1024]{2,0,1:T(8,128)S(1)} %get-tuple-element.61, ...), kind=kLoop, calls=%fused_computation.113 | loop fusion | flops 2850816 | bytes 2886144 | tf_op jit(solution)/shard_map/add | solution.py:147
  108.8 0.7 copy.65
  109.5 0.7 copy.66
  (52 shorter events, 12.8 us)
Async XLA Ops:
  1.6 100.6 %collective-permute-start.5 = (f32[8,4,1024]{2,0,1:T(8,128)S(1)}, f32[8,4,1024]{2,0,1:T(8,128)S(1)}, u32[]{:S(2)}, u32[]{:S(2)}) collective-permute-start(f32[8,4,1024]{2,0,1:T(8,128)S(1)} %get-tuple-element.61), channel_id=1, source_target_pairs={{0,1},{1,2},{2,3},{3,4},{4,5},{5,6},{6,7},{7,8},{8,9},{9,10},{10,1... | collective-permute-start | bytes 393224 | tf_op jit(solution)/shard_map/ppermute | solution.py:25
  6.5 95.8 %collective-permute-start.4 = (f32[8,4,1024]{2,0,1:T(8,128)S(1)}, f32[8,4,1024]{2,0,1:T(8,128)S(1)}, u32[]{:S(2)}, u32[]{:S(2)}) collective-permute-start(f32[8,4,1024]{2,0,1:T(8,128)S(1)} %get-tuple-element.61), channel_id=1, source_target_pairs={{1,0},{2,1},{3,2},{4,3},{5,4},{6,5},{7,6},{8,7},{9,8},{10,9},{11,1... | collective-permute-start | bytes 393224 | tf_op jit(solution)/shard_map/ppermute | solution.py:26
  24.1 19.1 %copy-start.2 = (s32[8]{0:T(128)S(1)}, s32[8]{0:T(128)}, u32[]{:S(2)}) copy-start(s32[8]{0:T(128)} %param.13) | copy-start | bytes 100
  24.1 21.2 %all-to-all-start = ((f32[3,2,1,64,128]{4,0,2,1,3:T(4,128)}), f32[3,2,1,64,128]{4,0,2,1,3:T(4,128)S(1)}, u32[]{:S(2)}, u32[]{:S(2)}) async-start(f32[3,2,1,64,128]{4,0,2,1,3:T(4,128)} %copy.48), calls=%async_computation | async-start | bytes 524288 | tf_op jit(solution)/shard_map/all_to_all | solution.py:92
  29.5 62.4 %collective-permute-start = (f32[8,4,4]{2,0,1:T(8,128)S(1)}, f32[8,4,4]{2,0,1:T(8,128)S(1)}, u32[]{:S(2)}, u32[]{:S(2)}) collective-permute-start(f32[8,4,4]{2,0,1:T(8,128)S(1)} %get-tuple-element.64), channel_id=1, source_target_pairs={{128,0},{256,128},{384,256},{512,384},{640,512},{768,640},{896,768... | collective-permute-start | bytes 1544 | tf_op jit(solution)/shard_map/ppermute | solution.py:26
  34.9 63.2 %collective-permute-start.1 = (f32[8,4,4]{2,0,1:T(8,128)S(1)}, f32[8,4,4]{2,0,1:T(8,128)S(1)}, u32[]{:S(2)}, u32[]{:S(2)}) collective-permute-start(f32[8,4,4]{2,0,1:T(8,128)S(1)} %get-tuple-element.65), channel_id=1, source_target_pairs={{0,128},{128,256},{256,384},{384,512},{512,640},{640,768},{768,896... | collective-permute-start | bytes 1544 | tf_op jit(solution)/shard_map/ppermute | solution.py:25
  36.8 61.4 %collective-permute-start.3 = (f32[4,4,1024]{2,0,1:T(4,128)S(1)}, f32[4,4,1024]{2,0,1:T(4,128)S(1)}, u32[]{:S(2)}, u32[]{:S(2)}) collective-permute-start(f32[4,4,1024]{2,0,1:T(4,128)S(1)} %get-tuple-element.62), channel_id=1, source_target_pairs={{0,16},{16,32},{32,48},{48,64},{64,80},{80,96},{96,112},{112,0},{1... | collective-permute-start | bytes 196616 | tf_op jit(solution)/shard_map/ppermute | solution.py:25
  51.0 0.7 copy-start.3
  85.5 16.9 %all-to-all-start.1 = ((f32[8,3,1,4,768]{4,3,1,2,0:T(4,128)}), f32[8,3,1,4,768]{4,3,1,2,0:T(4,128)S(1)}, u32[]{:S(2)}, u32[]{:S(2)}) async-start(f32[8,3,1,4,768]{4,3,1,2,0:T(4,128)} %bitcast.22), calls=%async_computation.1 | async-start | bytes 589824 | tf_op jit(solution)/shard_map/all_to_all | solution.py:103
  91.9 10.2 %collective-permute-start.2 = (f32[4,4,1024]{2,0,1:T(4,128)S(1)}, f32[4,4,1024]{2,0,1:T(4,128)S(1)}, u32[]{:S(2)}, u32[]{:S(2)}) collective-permute-start(f32[4,4,1024]{2,0,1:T(4,128)S(1)} %get-tuple-element.63), channel_id=1, source_target_pairs={{16,0},{32,16},{48,32},{64,48},{80,64},{96,80},{112,96},{0,112},{1... | collective-permute-start | bytes 196616 | tf_op jit(solution)/shard_map/ppermute | solution.py:26
  102.5 5.1 %copy-start = (f32[8,4,1024]{2,1,0:T(4,128)S(1)}, f32[8,4,1024]{2,1,0:T(4,128)}, u32[]{:S(2)}) copy-start(f32[8,4,1024]{2,1,0:T(4,128)} %param.10) | copy-start | bytes 393220
  102.5 5.1 %copy-start.1 = (f32[8,4,1024]{2,1,0:T(4,128)S(1)}, f32[8,4,1024]{2,1,0:T(4,128)}, u32[]{:S(2)}) copy-start(f32[8,4,1024]{2,1,0:T(4,128)} %param.11) | copy-start | bytes 393220
where the time goes:
time: 111 us; the launch traced here: 110 us
  starting transfers between devices  50.5 us (45%)
  local copies, waits for them, and re-layouts  17.5 us (16%)
  other arithmetic  13.9 us (13%)
  loops' own time  13.4 us (12%)
  matrix products  10.2 us (9%)
  waiting for transfers between devices  3.8 us (3%)
    ppermute x3, starting transfers between devices, padded_2(): lax.ppermute(leading, axis, [(b, a) for a, b in up])  27.4 us
    another operation x1, loops' own time, body(): pieces = lax.map(cut_block, block_numbers)  13.4 us
    ppermute x3, starting transfers between devices, padded_2(): lax.ppermute(last, axis, up)  12.6 us
    reduce_sum x9, other arithmetic, pick_entry(): jnp.sum(jnp.where(jnp.arange(table.shape[0], dtype=jnp.int32) == entry, t...  10.8 us
    dot_general x7, matrix products, contract(): jnp.einsum(pattern, first_term, second_term, precision=lax.Precision.HIGH...  10.2 us
    dynamic_update_slice x8, local copies, waits for them, and re-layouts, body(): pieces = lax.map(cut_block, block_numbers)  5.66 us
    all_to_all x1, starting transfers between devices, body(): lax.all_to_all(spectrum, 'gz', split_axis=3, concat_axis=4, tiled=True)  5.31 us
    all_to_all x1, starting transfers between devices, body(): lax.all_to_all(pieces, 'gx', split_axis=0, concat_axis=2, tiled=True)[0]  5.12 us
  transfers between devices with their start and end apart: 8, of which 1 were waited for; matrix products, arithmetic and copies ran while one was open for 29% of the time, Pallas kernels for 0%

commit v1 on v0

v1 whole, which is shorter than its diff:
```python
import functools
import math

import jax
import jax.numpy as jnp
import numpy as np
from jax import lax
from jax.experimental import pallas as pl
from jax.experimental.pallas import tpu as pltpu
from jax.sharding import PartitionSpec as P

first_coeffs = (0.8, -0.2, 4.0 / 105.0, -1.0 / 280.0)
second_coeffs = (1.6, -0.2, 8.0 / 315.0, -1.0 / 560.0)
center_coeff = -205.0 / 72.0
diffusivity = 0.15
time_step = 0.4
section_keep = -5.0 / 9.0
section_gain = 15.0 / 16.0

LANES = 128
LOW = 32
SEGMENT = 6
WINDOW = 8
VMEM_LIMIT = 16 * 1024 * 1024


def halves(values):
    high = values.astype(jnp.bfloat16)
    return high, (values - high.astype(jnp.float32)).astype(jnp.bfloat16)


def numpy_halves(values):
    values = values.astype(np.float32)
    high = values.astype(jnp.bfloat16)
    return high, (values - high.astype(np.float32)).astype(jnp.bfloat16)


def dot(a, b):
    return jnp.dot(a, b, preferred_element_type=jnp.float32)


@functools.cache
def tables():
    j = np.arange(LANES)
    h, g = np.meshgrid(np.arange(4), np.arange(16), indexing="ij")
    angle = 2 * math.pi * (((4 * g + h)[:, :, None] * j) % LANES) / LANES
    real_rows = np.concatenate([np.cos(angle), np.sin(angle)], -1)
    imag_rows = np.concatenate([-np.sin(angle), np.cos(angle)], -1)
    first = np.stack([real_rows, imag_rows], 1).reshape(LANES, 2 * LANES)
    first_high, first_low = numpy_halves(first)
    low = np.arange(LOW)
    twist = 2 * math.pi * (low[:, None] * j[None, :]) / (LOW * LANES)
    twiddle = np.stack([np.cos(twist), np.sin(twist)]).astype(np.float32)
    m = np.arange(LOW)[:, None, None] + np.arange(WINDOW)[:, None]
    last_angle = 2 * math.pi * ((m * low) % LOW) / LOW
    last = np.concatenate([np.cos(last_angle), -np.sin(last_angle)], -1)
    last_high, last_low = (t.astype(np.float32) for t in numpy_halves(last))
    last_all = np.concatenate([last_high, last_low, last_high], -1)
    return np.concatenate([first_high, first_high, first_low], 0), twiddle, last_all


def pack_kernel(spectrum_ref, theta_ref, out_ref, low_ref, high_ref, got, packed, sems):
    groups, dests, rows = 2, out_ref.shape[0], theta_ref.shape[0]
    count = dests // groups
    heads = [
        pltpu.make_async_copy(
            spectrum_ref.at[:, pl.ds(4 * count * group, 4 * count), :],
            got.at[:, pl.ds(4 * count * group, 4 * count), :],
            sems.at[group],
        )
        for group in range(groups)
    ]
    tails = [
        pltpu.make_async_copy(
            packed.at[pl.ds(count * group, count)],
            out_ref.at[pl.ds(count * group, count)],
            sems.at[groups + group],
        )
        for group in range(groups)
    ]
    sides = [
        pltpu.make_async_copy(theta_ref.at[pl.ds(0, 4)], low_ref, sems.at[2 * groups]),
        pltpu.make_async_copy(theta_ref.at[pl.ds(rows - 4, 4)], high_ref, sems.at[2 * groups + 1]),
    ]
    for copy in heads + sides:
        copy.start()
    for group in range(groups):
        heads[group].wait()
        for dest in range(count * group, count * (group + 1)):
            for part in range(6):
                packed[dest, 4 * part : 4 * part + 4, :] = got[part, 4 * dest : 4 * dest + 4, :]
        tails[group].start()
    for copy in tails + sides:
        copy.wait()


def edges_of(theta_ref):
    spot = lax.broadcasted_iota(jnp.int32, (8, LANES), 1)
    edges = jnp.zeros((8, LANES), jnp.float32)
    cells = theta_ref.shape[2]
    for z in range(4):
        tail = pltpu.roll(theta_ref[:, z, cells - LANES :], (8 * z + 4) % LANES, 1)
        head = pltpu.roll(theta_ref[:, z, :LANES], 8 * z + 4, 1)
        edges = jnp.where((spot >= 8 * z) & (spot < 8 * z + 4), tail, edges)
        edges = jnp.where((spot >= 8 * z + 4) & (spot < 8 * z + 8), head, edges)
    return edges


def setup_kernel(
    offset_hbm, theta_hbm, last_hbm, first_hbm, twiddle_hbm,
    left_ref, turn_ref, edges_ref, first_ref, twiddle_ref,
    offset, theta, last, sems,
):
    moves = ((offset_hbm, offset), (theta_hbm, theta), (last_hbm, last))
    moves += ((first_hbm, first_ref), (twiddle_hbm, twiddle_ref))
    copies = [
        pltpu.make_async_copy(source, target, sems.at[number])
        for number, (source, target) in enumerate(moves)
    ]
    for copy in copies:
        copy.start()
    for copy in copies:
        copy.wait()
    blocks = left_ref.shape[0] // WINDOW
    left = [last[offset[block] // LANES] for block in range(blocks)]
    left_ref[...] = jnp.concatenate(left, 0).astype(jnp.bfloat16)
    lane = lax.broadcasted_iota(jnp.int32, (1, LANES), 1)
    for block in range(blocks):
        turn_ref[block : block + 1, :] = jnp.where(lane < offset[block] % LANES, 1.0, 0.0)
    edges_ref[...] = edges_of(theta)


def fill_matrix(start, length, index_ref, weight_ref, matrix, matrix_ref, sems):
    rows = lax.broadcasted_iota(jnp.int32, (8, LANES), 0)
    taps = index_ref.shape[0]
    copies = []
    for pair in range(matrix.shape[0]):
        for side in range(2):
            lanes = slice((2 * pair + side) * LANES, (2 * pair + side + 1) * LANES)
            index = index_ref[:, lanes]
            weight = jnp.where(index < length, weight_ref[:, lanes], 0.0)
            inner = lax.rem(index + start, LANES)
            spots = [jnp.broadcast_to(inner[t : t + 1], (8, LANES)) for t in range(taps)]
            parts = []
            for m in range(SEGMENT):
                part = jnp.where(index // LANES == m, weight, 0.0)
                parts.append([jnp.broadcast_to(part[t : t + 1], (8, LANES)) for t in range(taps)])

            def step(number, carry, side=side, pair=pair, spots=spots, parts=parts):
                near = [rows + 16 * number, rows + (16 * number + 8)]
                hits = [[near[half] == spots[t] for t in range(taps)] for half in range(2)]
                for m in range(SEGMENT):
                    total = []
                    for half in range(2):
                        terms = [jnp.where(hits[half][t], parts[m][t], 0.0) for t in range(taps)]
                        while len(terms) > 1:
                            terms = [a + b for a, b in zip(terms[::2], terms[1::2], strict=True)]
                        total.append(terms[0])
                    high, low = halves(jnp.concatenate(total, 0))
                    at = pl.ds(pl.multiple_of(LANES * m + 16 * number, 16), 16)
                    matrix[pair, 0, at, side * LANES : (side + 1) * LANES] = high
                    matrix[pair, 1, at, side * LANES : (side + 1) * LANES] = low
                return carry

            lax.fori_loop(0, LANES // 16, step, 0)
        copies.append(pltpu.make_async_copy(matrix.at[pair], matrix_ref.at[pair], sems.at[pair]))
        copies[-1].start()
    return copies


def transform_kernel(
    got_ref, first_ref, twiddle_ref, left_ref, turn_ref, edges_ref, *after_and_out
):
    out_ref = after_and_out[-1]
    lane = lax.broadcasted_iota(jnp.int32, (LOW, LANES), 1) // LOW
    pieces = []
    for comp in range(3):
        rows = [
            got_ref[pl.ds(comp * 8 + part * 4 + z, 16, stride=24), :]
            for z in range(4)
            for part in range(2)
        ]
        turned = jnp.concatenate(rows, 0).T
        for z in range(4):
            piece = jnp.zeros((LOW, LANES), jnp.float32)
            for h in range(4):
                moved = turned[LOW * h : LOW * (h + 1), :]
                if h != z:
                    moved = pltpu.roll(moved, (LOW * (h - z)) % LANES, 1)
                piece = jnp.where(lane == h, moved, piece)
            pieces.append(piece)
    high, low = halves(jnp.concatenate(pieces, 0))
    done = dot(jnp.concatenate([high, low], 1), first_ref[: 2 * LANES, :]) + dot(
        high, first_ref[2 * LANES :, :]
    )
    cosine, sine = twiddle_ref[0], twiddle_ref[1]
    right = []
    for line in range(12):
        real = done[LOW * line : LOW * (line + 1), :LANES]
        imag = done[LOW * line : LOW * (line + 1), LANES:]
        high, low = halves(
            jnp.concatenate([real * cosine - imag * sine, real * sine + imag * cosine], 0)
        )
        right.append(jnp.concatenate([high, high, low], 0))
    lines = dot(left_ref[...], jnp.concatenate(right, 1))
    for block in range(out_ref.shape[0]):
        turned = jnp.broadcast_to(turn_ref[block : block + 1, :], (WINDOW, LANES)) > 0.5
        for line in range(12):
            cells = lines[WINDOW * block : WINDOW * (block + 1), line * LANES : (line + 1) * LANES]
            out_ref[block, line] = jnp.where(turned, pltpu.roll(cells, WINDOW - 1, 0), cells)
    for block in range(out_ref.shape[0]):
        for y in range(8):
            out_ref[block, y, WINDOW - 1 :, :] = edges_ref[y : y + 1]


def local_kernel(
    z_low_ref, z_high_ref, y_low_ref, y_high_ref,
    theta_hbm, sum_hbm, offset_hbm, length_hbm, index_hbm, weight_hbm, after_ref,
    out_ref, matrix_ref,
    theta, sums, offset, length, index, weight, matrix, sems, out_sems,
):
    block = lax.axis_index("gx")
    cells = theta.shape[2]
    mine = pl.ds(pl.multiple_of(block * cells, LANES), cells)
    moves = ((offset_hbm, offset), (length_hbm, length))
    moves += ((index_hbm.at[:, mine], index), (weight_hbm.at[:, mine], weight))
    moves += ((theta_hbm, theta), (sum_hbm, sums))
    copies = [
        pltpu.make_async_copy(source, target, sems.at[number])
        for number, (source, target) in enumerate(moves)
    ]
    for copy in copies:
        copy.start()
    for copy in copies[:4]:
        copy.wait()
    tails = fill_matrix(offset[block], length[block], index, weight, matrix, matrix_ref, out_sems)
    for copy in copies[4:]:
        copy.wait()
    stencil(theta, sums, z_low_ref, z_high_ref, y_low_ref, y_high_ref, out_ref)
    for copy in tails:
        copy.wait()


def stencil(theta_ref, sum_ref, z_low_ref, z_high_ref, y_low_ref, y_high_ref, out_ref):
    cells = theta_ref.shape[2]
    lane = lax.broadcasted_iota(jnp.int32, (8, cells), 1)
    planes = [ref[:, z, :] for ref in (z_low_ref, theta_ref, z_high_ref) for z in range(4)]
    for z in range(4):
        here = planes[4 + z]
        column = jnp.concatenate([y_low_ref[:, z, :], here, y_high_ref[:, z, :]], 0)
        grad_x = jnp.zeros_like(here)
        grad_y = jnp.zeros_like(here)
        grad_z = jnp.zeros_like(here)
        laplace = 3.0 * center_coeff * here
        for reach in range(1, 5):
            first = -time_step * first_coeffs[reach - 1]
            ahead_x = jnp.where(lane < cells - reach, pltpu.roll(here, cells - reach, 1), 0.0)
            behind_x = jnp.where(lane >= reach, pltpu.roll(here, reach, 1), 0.0)
            ahead_y = column[4 + reach : 12 + reach]
            behind_y = column[4 - reach : 12 - reach]
            ahead_z = planes[4 + z + reach]
            behind_z = planes[4 + z - reach]
            grad_x = grad_x + first * (ahead_x - behind_x)
            grad_y = grad_y + first * (ahead_y - behind_y)
            grad_z = grad_z + first * (ahead_z - behind_z)
            laplace = laplace + second_coeffs[reach - 1] * (
                (ahead_x + behind_x) + (ahead_y + behind_y) + (ahead_z + behind_z)
            )
        out_ref[0, z] = grad_x
        out_ref[1, z] = grad_y
        out_ref[2, z] = grad_z
        out_ref[3, z] = section_keep * sum_ref[:, z, :] + (time_step * diffusivity) * laplace
        out_ref[4, z] = here


def combine_kernel(
    got_ref, matrix_hbm, local_ref, theta_ref, section_ref, matrix_ref, sems
):
    copies = [
        pltpu.make_async_copy(matrix_hbm.at[pair], matrix_ref.at[pair], sems.at[pair])
        for pair in range(matrix_ref.shape[0])
    ]
    for copy in copies:
        copy.start()
    block = lax.axis_index("gx")
    blocks = got_ref.shape[0] // (12 * WINDOW)
    cells = local_ref.shape[3]
    rows = [
        jnp.concatenate(
            [
                got_ref[pl.ds(WINDOW * line + m, blocks, stride=12 * WINDOW), :]
                for line in range(12)
            ],
            0,
        )
        for m in range(SEGMENT)
    ]
    high, low = halves(jnp.concatenate(rows, 1))
    both = jnp.concatenate([high, low], 0)
    count = high.shape[0]

    def halo_of(source):
        return got_ref[pl.ds(source * 12 * WINDOW + WINDOW - 1, 8, stride=WINDOW), :]

    before = halo_of(lax.rem(block + blocks - 1, blocks))
    after = halo_of(lax.rem(block + 1, blocks))
    lane = lax.broadcasted_iota(jnp.int32, (8, LANES), 1)
    width = 2 * LANES
    for tile in range(cells // width):
        lanes = slice(tile * width, (tile + 1) * width)
        copies[tile].wait()
        twice = dot(both, matrix_ref[tile, 0])
        carried = twice[:count] + twice[count:] + dot(high, matrix_ref[tile, 1])
        for z in range(4):
            grad_x = local_ref[0, z, :, lanes]
            base = local_ref[3, z, :, lanes]
            if tile == 0 or (tile + 1) * width == cells:
                more_grad = jnp.zeros((8, LANES), jnp.float32)
                more_base = jnp.zeros((8, LANES), jnp.float32)
                for reach in range(1, 5):
                    if tile == 0:
                        moved = pltpu.roll(before, (LANES - 4 - 8 * z + reach) % LANES, 1)
                        halo = jnp.where(lane < reach, moved, 0.0)
                        sign = 1.0
                    else:
                        moved = pltpu.roll(after, (LANES - 4 - 8 * z - reach) % LANES, 1)
                        halo = jnp.where(lane >= LANES - reach, moved, 0.0)
                        sign = -1.0
                    more_grad = more_grad + (sign * time_step * first_coeffs[reach - 1]) * halo
                    more_base = (
                        more_base + (time_step * diffusivity * second_coeffs[reach - 1]) * halo
                    )
                none = jnp.zeros((8, LANES), jnp.float32)
                order = (lambda v: [v, none]) if tile == 0 else (lambda v: [none, v])
                grad_x = grad_x + jnp.concatenate(order(more_grad), 1)
                base = base + jnp.concatenate(order(more_base), 1)
            section = (
                base
                + carried[8 * z : 8 * z + 8] * grad_x
                + carried[32 + 8 * z : 40 + 8 * z] * local_ref[1, z, :, lanes]
                + carried[64 + 8 * z : 72 + 8 * z] * local_ref[2, z, :, lanes]
            )
            section_ref[:, z, lanes] = section
            theta_ref[:, z, lanes] = local_ref[4, z, :, lanes] + section_gain * section


def f32(*shape):
    return jax.ShapeDtypeStruct(shape, jnp.float32)


def bf16(*shape):
    return jax.ShapeDtypeStruct(shape, jnp.bfloat16)


VMEM = pl.BlockSpec(memory_space=pltpu.VMEM)
HBM = pl.BlockSpec(memory_space=pltpu.HBM)
ANY = pl.BlockSpec(memory_space=pl.ANY)


def in_hbm(array):
    return pltpu.with_memory_space_constraint(array, pltpu.HBM)


def run(kernel, name, in_specs, outs, scratch=()):
    return pl.pallas_call(
        kernel,
        out_shape=tuple(shape for shape, _ in outs),
        in_specs=in_specs,
        out_specs=tuple(spec for _, spec in outs),
        scratch_shapes=scratch,
        compiler_params=pltpu.CompilerParams(vmem_limit_bytes=VMEM_LIMIT),
        cost_estimate=pl.CostEstimate(flops=4 * 10**9, bytes_accessed=4 * 10**6, transcendentals=0),
        name=name,
    )


def neighbours(edge_low, edge_high, axis):
    count = lax.axis_size(axis)
    up = [(i, (i + 1) % count) for i in range(count)]
    return lax.ppermute(edge_high, axis, up), lax.ppermute(edge_low, axis, [(b, a) for a, b in up])


def body(spectrum, theta, section_sum, seg_offset, seg_length, stencil_index, stencil_weight):
    blocks, depth = lax.axis_size("gx"), lax.axis_size("gz")
    rows_count, layers, cells = theta.shape
    taps = stencil_index.shape[0]
    first, twiddle, last = (jnp.asarray(t) for t in tables())
    vmem, smem, dma = pltpu.VMEM, pltpu.SMEM, pltpu.SemaphoreType.DMA

    edge = f32(4, layers, cells)
    packed, y_first, y_last = run(
        pack_kernel,
        "pack",
        [HBM, HBM],
        [(f32(depth, 24, LANES), HBM), (edge, HBM), (edge, HBM)],
        [vmem((6, 4 * depth, LANES), jnp.float32), vmem((depth, 24, LANES), jnp.float32), dma((6,))],
    )(in_hbm(spectrum.reshape(6, 4 * depth, LANES)), in_hbm(theta))
    columns = lax.all_to_all(packed, "gz", split_axis=0, concat_axis=0, tiled=True)
    z_low, z_high = neighbours(theta, theta, "gz")
    y_low, y_high = neighbours(y_first, y_last, "gy")
    left, turn, edges, first, twiddle = run(
        setup_kernel,
        "setup",
        [HBM] * 5,
        [
            (bf16(blocks * WINDOW, last.shape[2]), VMEM),
            (f32(blocks, LANES), VMEM),
            (f32(8, LANES), VMEM),
            (bf16(*first.shape), VMEM),
            (f32(*twiddle.shape), VMEM),
        ],
        [smem((blocks,), jnp.int32), vmem(theta.shape, jnp.float32), vmem(last.shape, jnp.float32)]
        + [dma((5,))],
    )(seg_offset, theta, last, first, twiddle)
    (pieces,) = run(
        transform_kernel,
        "transform",
        [VMEM] * 6 + [ANY] * 4,
        [(f32(blocks, 12, WINDOW, LANES), VMEM)],
    )(
        columns.reshape(depth * 24, LANES), first, twiddle, left, turn, edges,
        z_low, z_high, y_low, y_high,
    )
    arrived = lax.all_to_all(pieces, "gx", split_axis=0, concat_axis=0, tiled=True)
    matrix_shape = (cells // (2 * LANES), 2, SEGMENT * LANES, 2 * LANES)
    local, matrix = run(
        local_kernel,
        "local",
        [VMEM] * 4 + [HBM] * 6 + [ANY],
        [(f32(5, layers, rows_count, cells), VMEM), (pltpu.HBM(matrix_shape, jnp.bfloat16), HBM)],
        [vmem(theta.shape, jnp.float32), vmem(theta.shape, jnp.float32)]
        + [smem((blocks,), jnp.int32), smem((blocks,), jnp.int32)]
        + [vmem((taps, cells), jnp.int32), vmem((taps, cells), jnp.float32)]
        + [vmem(matrix_shape, jnp.bfloat16), dma((6,)), dma((matrix_shape[0],))],
    )(
        z_low, z_high, y_low, y_high,
        theta, section_sum, seg_offset, seg_length, stencil_index, stencil_weight, pieces,
    )
    matrix = in_hbm(matrix)
    return run(
        combine_kernel,
        "combine",
        [VMEM, HBM, VMEM],
        [(f32(*theta.shape), VMEM), (f32(*theta.shape), VMEM)],
        [vmem(matrix_shape, jnp.bfloat16), dma((matrix_shape[0],))],
    )(arrived.reshape(blocks * 12 * WINDOW, LANES), matrix, local)


def solution(mesh):
    placed = (
        P(None, None, ("gy", "gx"), None, "gz"),
        P("gy", "gz", "gx"),
        P("gy", "gz", "gx"),
        P(),
        P(),
        P(),
        P(),
    )
    return jax.shard_map(
        body,
        mesh=mesh,
        in_specs=placed,
        out_specs=(P("gy", "gz", "gx"), P("gy", "gz", "gx")),
        check_vma=False,
    )
```

time: 111 us -> 60.1 us (0.54)
  the two profiles are of different devices: /device:TPU:1 before, /device:TPU:17 now
where the time goes in v1:
time: 60.1 us; the launch traced here: 59.7 us
  starting transfers between devices  37.9 us (63%)
  Pallas kernels  12.5 us (21%)
  waiting for transfers between devices  8.42 us (14%)
  between operations  0.85 us (1%)
    all_to_all x1, starting transfers between devices, body(): lax.all_to_all(packed, 'gz', split_axis=0, concat_axis=0, tiled=True)  18.6 us
    ppermute x2, starting transfers between devices, neighbours(): lax.ppermute(edge_high, axis, up)  10.1 us
    ppermute x2, waiting for transfers between devices, neighbours(): lax.ppermute(edge_low, axis, [(b, a) for a, b in up])  5.72 us
    ppermute x2, starting transfers between devices, neighbours(): lax.ppermute(edge_low, axis, [(b, a) for a, b in up])  5.14 us
    pallas_call x1, Pallas kernels, body(): run(local_kernel, 'local', [VMEM] * 4 + [HBM] * 6 + [ANY], [(f32(5, layer...  5.01 us
    all_to_all x1, starting transfers between devices, body(): lax.all_to_all(pieces, 'gx', split_axis=0, concat_axis=0, tiled=True)  4.02 us
    pallas_call x1, Pallas kernels, body(): run(combine_kernel, 'combine', [VMEM, HBM, VMEM], [(f32(*theta.shape), VM...  3.54 us
    all_to_all x1, waiting for transfers between devices, body(): lax.all_to_all(pieces, 'gx', split_axis=0, concat_axis=0, tiled=True)  2.69 us
  transfers between devices with their start and end apart: 6, of which 2 were waited for; matrix products, arithmetic and copies ran while one was open for 0% of the time, Pallas kernels for 10%

profile of v1, /device:TPU:17, one launch (start us, length us, event | category | flops | bytes accessed | tf_op | source)
XLA Modules:
  0.0 59.7 jit_solution(14801983132810058634)
XLA Ops:
  0.6 0.0 copy-start.2
  0.6 0.0 copy-start.4
  0.6 0.0 copy-start.6
  0.7 0.0 copy-start.7
  0.7 0.0 copy-start.8
  0.7 1.7 %pack.1 = (f32[16,24,128]{2,1,0:T(8,128)}, f32[4,4,1024]{2,1,0:T(4,128)S(1)}, f32[4,4,1024]{2,1,0:T(4,128)S(1)}) custom-call(f32[6,64,128]{2,1,0:T(8,128)} %bitcast.5, f32[8,4,1024]{2,1,0:T(4,128)} %theta_hbm.3), custom_call_target="tpu_custom_call" | custom-call | flops 4000000000 | bytes 4000000 | tf_op jit(solution)/shard_map/pack/pallas_call | solution.py:391
  2.4 18.6 %all-to-all-start = ((f32[16,24,128]{2,1,0:T(8,128)}), f32[16,24,128]{2,1,0:T(8,128)S(1)}, u32[]{:S(2)}, u32[]{:S(2)}) async-start(f32[16,24,128]{2,1,0:T(8,128)} %get-tuple-element.12), calls=%async_computation | async-start | bytes 393216 | tf_op jit(solution)/shard_map/all_to_all | solution.py:398
  21.0 0.0 copy-done.2
  21.0 3.3 %collective-permute-start = (f32[8,4,1024]{2,1,0:T(4,128)S(1)}, f32[8,4,1024]{2,1,0:T(4,128)S(1)}, u32[]{:S(2)}, u32[]{:S(2)}) collective-permute-start(f32[8,4,1024]{2,1,0:T(4,128)S(1)} %copy-done.2), channel_id=1, source_target_pairs={{0,1},{1,2},{2,3},{3,4},{4,5},{5,6},{6,7},{7,8},{8,9},{9,10},{10,1... | collective-permute-start | bytes 393224 | tf_op jit(solution)/shard_map/ppermute | solution.py:380
  24.3 3.2 %collective-permute-start.1 = (f32[8,4,1024]{2,1,0:T(4,128)S(1)}, f32[8,4,1024]{2,1,0:T(4,128)S(1)}, u32[]{:S(2)}, u32[]{:S(2)}) collective-permute-start(f32[8,4,1024]{2,1,0:T(4,128)S(1)} %copy-done.2), channel_id=1, source_target_pairs={{1,0},{2,1},{3,2},{4,3},{5,4},{6,5},{7,6},{8,7},{9,8},{10,9},{11,1... | collective-permute-start | bytes 393224 | tf_op jit(solution)/shard_map/ppermute | solution.py:380
  27.5 6.8 %collective-permute-start.2 = (f32[4,4,1024]{2,1,0:T(4,128)S(1)}, f32[4,4,1024]{2,1,0:T(4,128)S(1)}, u32[]{:S(2)}, u32[]{:S(2)}) collective-permute-start(f32[4,4,1024]{2,1,0:T(4,128)S(1)} %get-tuple-element.18), channel_id=1, source_target_pairs={{0,16},{16,32},{32,48},{48,64},{64,80},{80,96},{96,112},{112,0},{1... | collective-permute-start | bytes 196616 | tf_op jit(solution)/shard_map/ppermute | solution.py:380
  34.4 1.9 %collective-permute-start.3 = (f32[4,4,1024]{2,1,0:T(4,128)S(1)}, f32[4,4,1024]{2,1,0:T(4,128)S(1)}, u32[]{:S(2)}, u32[]{:S(2)}) collective-permute-start(f32[4,4,1024]{2,1,0:T(4,128)S(1)} %get-tuple-element.19), channel_id=1, source_target_pairs={{16,0},{32,16},{48,32},{64,48},{80,64},{96,80},{112,96},{0,112},{1... | collective-permute-start | bytes 196616 | tf_op jit(solution)/shard_map/ppermute | solution.py:380
  36.3 0.0 copy-done.4
  36.3 0.0 copy-done.6
  36.3 0.0 copy-done.7
  36.3 0.0 copy-done.8
  36.3 0.7 %setup.1 = (bf16[64,192]{1,0:T(8,128)(2,1)S(1)}, f32[8,128]{1,0:T(8,128)S(1)}, f32[8,128]{1,0:T(8,128)S(1)}, bf16[384,256]{1,0:T(8,128)(2,1)S(1)}, f32[2,32,128]{2,1,0:T(8,128)S(1)}) custom-call(s32[8]{0:T(128)S(1)} %copy-done.4, f32[8,4,1024]{2,1,0:T(4,128)S(1)} %copy-done.2, f32[32,8,192]{2,1,0:T(8,128)S(1)} %copy-done.6, bf16[384,256]{1,0:T(8,128)(2,1)S(1)} %copy-done.7, ...), custom_call_target="tpu_custom_call" | custom-call | flops 4000000000 | bytes 4000000 | tf_op jit(solution)/shard_map/setup/pallas_call | solution.py:401
  37.0 0.0 collective-permute-done.2.after_and_out_2_.y_low_ref
  37.0 5.7 %collective-permute-done.3.after_and_out_3_.y_high_ref = f32[4,4,1024]{2,1,0:T(4,128)S(1)} collective-permute-done((f32[4,4,1024]{2,1,0:T(4,128)S(1)}, f32[4,4,1024]{2,1,0:T(4,128)S(1)}, u32[]{:S(2)}, u32[]{:S(2)}) %collective-permute-start.3) | collective-permute-done | bytes 65568 | tf_op jit(solution)/shard_map/ppermute | solution.py:380
  42.8 0.0 collective-permute-done.after_and_out_0_.z_low_ref
  42.8 0.0 collective-permute-done.1.after_and_out_1_.z_high_ref
  42.8 0.0 all-to-all-done
  42.8 0.0 copy-start
  42.8 0.0 copy-start.1
  42.8 0.0 copy-start.3
  42.8 0.0 copy-start.5
  42.8 1.5 %transform.1.after_ref = f32[8,12,8,128]{3,2,1,0:T(8,128)} custom-call(f32[384,128]{1,0:T(8,128)S(1)} %bitcast.4, bf16[384,256]{1,0:T(8,128)(2,1)S(1)} %get-tuple-element.13.first_ref, f32[2,32,128]{2,1,0:T(8,128)S(1)} %get-tuple-element.14.twiddle_ref, bf16[64,192]{1,0:T(8,128)(2,1)S(1)} %get-tuple-element.15.left_ref, ...), custom_call_target="tpu_custom_call" | custom-call | flops 4000000000 | bytes 4000000 | tf_op jit(solution)/shard_map/transform/pallas_call | solution.py:415
  44.4 4.0 %all-to-all-start.1 = ((f32[8,12,8,128]{3,2,1,0:T(8,128)}), f32[8,12,8,128]{3,2,1,0:T(8,128)S(1)}, u32[]{:S(2)}, u32[]{:S(2)}) async-start(f32[8,12,8,128]{3,2,1,0:T(8,128)} %transform.1.after_ref), calls=%async_computation.1 | async-start | bytes 786432 | tf_op jit(solution)/shard_map/all_to_all | solution.py:424
  48.4 0.0 copy-done
  48.4 5.0 %local.1 = (f32[5,4,8,1024]{3,2,1,0:T(8,128)S(1)}, bf16[4,2,768,256]{3,2,1,0:T(8,128)(2,1)}) custom-call(f32[8,4,1024]{2,1,0:T(4,128)S(1)} %collective-permute-done.after_and_out_0_.z_low_ref, f32[8,4,1024]{2,1,0:T(4,128)S(1)} %collective-permute-done.1.after_and_out_1_.z_high_ref, f32[4,4,1024]{2,1,0:T(4,128)S(1)} %collective-permute-done.2.after_and_out_2_.y_low_ref, ...), custom_call_target="tpu_custom_call" | custom-call | flops 4000000000 | bytes 4000000 | tf_op jit(solution)/shard_map/local/pallas_call | solution.py:426
  53.4 2.7 %all-to-all-done.1 = f32[8,12,8,128]{3,2,1,0:T(8,128)S(1)} async-done(((f32[8,12,8,128]{3,2,1,0:T(8,128)}), f32[8,12,8,128]{3,2,1,0:T(8,128)S(1)}, u32[]{:S(2)}, u32[]{:S(2)}) %all-to-all-start.1) | async-done | bytes 393248 | tf_op jit(solution)/shard_map/all_to_all | solution.py:424
  56.1 3.5 %combine.1 = (f32[8,4,1024]{2,1,0:T(4,128)}, f32[8,4,1024]{2,1,0:T(4,128)}) custom-call(f32[768,128]{1,0:T(8,128)S(1)} %bitcast.3, bf16[4,2,768,256]{3,2,1,0:T(8,128)(2,1)} %get-tuple-element.20.matrix_hbm, f32[5,4,8,1024]{3,2,1,0:T(8,128)S(1)} %get-tuple-element.21.local_ref), custom_call_target="tpu_custom_call" | custom-call | flops 4000000000 | bytes 4000000 | tf_op jit(solution)/shard_map/combine/pallas_call | solution.py:440
  (3 shorter events, 0.0 us)
Async XLA Ops:
  0.6 20.4 %copy-start.2 = (f32[8,4,1024]{2,1,0:T(4,128)S(1)}, f32[8,4,1024]{2,1,0:T(4,128)}, u32[]{:S(2)}) copy-start(f32[8,4,1024]{2,1,0:T(4,128)} %theta_hbm.3) | copy-start | bytes 393220
  0.6 35.7 %copy-start.4 = (s32[8]{0:T(128)S(1)}, s32[8]{0:T(128)}, u32[]{:S(2)}) copy-start(s32[8]{0:T(128)} %offset_hbm.3) | copy-start | bytes 100
  0.6 35.7 %copy-start.6 = (f32[32,8,192]{2,1,0:T(8,128)S(1)}, f32[32,8,192]{2,1,0:T(8,128)}, u32[]{:S(2)}) copy-start(f32[32,8,192]{2,1,0:T(8,128)} %constant.8.clone.last_hbm) | copy-start | bytes 589828
  0.7 35.7 %copy-start.7 = (bf16[384,256]{1,0:T(8,128)(2,1)S(1)}, bf16[384,256]{1,0:T(8,128)(2,1)}, u32[]{:S(2)}) copy-start(bf16[384,256]{1,0:T(8,128)(2,1)} %constant.6.clone.first_hbm) | copy-start | bytes 589828
  0.7 35.7 %copy-start.8 = (f32[2,32,128]{2,1,0:T(8,128)S(1)}, f32[2,32,128]{2,1,0:T(8,128)}, u32[]{:S(2)}) copy-start(f32[2,32,128]{2,1,0:T(8,128)} %constant.7.clone.twiddle_hbm) | copy-start | bytes 98308
  2.4 40.4 %all-to-all-start = ((f32[16,24,128]{2,1,0:T(8,128)}), f32[16,24,128]{2,1,0:T(8,128)S(1)}, u32[]{:S(2)}, u32[]{:S(2)}) async-start(f32[16,24,128]{2,1,0:T(8,128)} %get-tuple-element.12), calls=%async_computation | async-start | bytes 393216 | tf_op jit(solution)/shard_map/all_to_all | solution.py:398
  21.0 21.7 %collective-permute-start = (f32[8,4,1024]{2,1,0:T(4,128)S(1)}, f32[8,4,1024]{2,1,0:T(4,128)S(1)}, u32[]{:S(2)}, u32[]{:S(2)}) collective-permute-start(f32[8,4,1024]{2,1,0:T(4,128)S(1)} %copy-done.2), channel_id=1, source_target_pairs={{0,1},{1,2},{2,3},{3,4},{4,5},{5,6},{6,7},{7,8},{8,9},{9,10},{10,1... | collective-permute-start | bytes 393224 | tf_op jit(solution)/shard_map/ppermute | solution.py:380
  24.3 18.5 %collective-permute-start.1 = (f32[8,4,1024]{2,1,0:T(4,128)S(1)}, f32[8,4,1024]{2,1,0:T(4,128)S(1)}, u32[]{:S(2)}, u32[]{:S(2)}) collective-permute-start(f32[8,4,1024]{2,1,0:T(4,128)S(1)} %copy-done.2), channel_id=1, source_target_pairs={{1,0},{2,1},{3,2},{4,3},{5,4},{6,5},{7,6},{8,7},{9,8},{10,9},{11,1... | collective-permute-start | bytes 393224 | tf_op jit(solution)/shard_map/ppermute | solution.py:380
  27.5 9.5 %collective-permute-start.2 = (f32[4,4,1024]{2,1,0:T(4,128)S(1)}, f32[4,4,1024]{2,1,0:T(4,128)S(1)}, u32[]{:S(2)}, u32[]{:S(2)}) collective-permute-start(f32[4,4,1024]{2,1,0:T(4,128)S(1)} %get-tuple-element.18), channel_id=1, source_target_pairs={{0,16},{16,32},{32,48},{48,64},{64,80},{80,96},{96,112},{112,0},{1... | collective-permute-start | bytes 196616 | tf_op jit(solution)/shard_map/ppermute | solution.py:380
  34.4 8.4 %collective-permute-start.3 = (f32[4,4,1024]{2,1,0:T(4,128)S(1)}, f32[4,4,1024]{2,1,0:T(4,128)S(1)}, u32[]{:S(2)}, u32[]{:S(2)}) collective-permute-start(f32[4,4,1024]{2,1,0:T(4,128)S(1)} %get-tuple-element.19), channel_id=1, source_target_pairs={{16,0},{32,16},{48,32},{64,48},{80,64},{96,80},{112,96},{0,112},{1... | collective-permute-start | bytes 196616 | tf_op jit(solution)/shard_map/ppermute | solution.py:380
  42.8 5.6 %copy-start = (s32[8,8192]{1,0:T(8,128)S(1)}, s32[8,8192]{1,0:T(8,128)}, u32[]{:S(2)}) copy-start(s32[8,8192]{1,0:T(8,128)} %index_hbm.1) | copy-start | bytes 786436
  42.8 5.6 %copy-start.1 = (f32[8,8192]{1,0:T(8,128)S(1)}, f32[8,8192]{1,0:T(8,128)}, u32[]{:S(2)}) copy-start(f32[8,8192]{1,0:T(8,128)} %weight_hbm.1) | copy-start | bytes 786436
  42.8 5.6 %copy-start.3 = (f32[8,4,1024]{2,1,0:T(4,128)S(1)}, f32[8,4,1024]{2,1,0:T(4,128)}, u32[]{:S(2)}) copy-start(f32[8,4,1024]{2,1,0:T(4,128)} %sum_hbm.1) | copy-start | bytes 393220
  42.8 5.6 %copy-start.5 = (s32[8]{0:T(128)S(1)}, s32[8]{0:T(128)}, u32[]{:S(2)}) copy-start(s32[8]{0:T(128)} %length_hbm.1) | copy-start | bytes 100
  44.4 11.8 %all-to-all-start.1 = ((f32[8,12,8,128]{3,2,1,0:T(8,128)}), f32[8,12,8,128]{3,2,1,0:T(8,128)S(1)}, u32[]{:S(2)}, u32[]{:S(2)}) async-start(f32[8,12,8,128]{3,2,1,0:T(8,128)} %transform.1.after_ref), calls=%async_computation.1 | async-start | bytes 786432 | tf_op jit(solution)/shard_map/all_to_all | solution.py:424

commit v2 on v1

--- a/solution.py
+++ b/solution.py
@@ -130,15 +130,36 @@
     edges_ref[...] = edges_of(theta)
 
 
-def fill_matrix(start, length, index_ref, weight_ref, matrix, matrix_ref, sems):
+def matrix_kernel(
+    offset_hbm, length_hbm, index_hbm, weight_hbm, after_ref,
+    near_ref, far_hbm,
+    offset, length, index_ref, weight_ref, far_ref, sems, out_sems,
+):
+    block = lax.axis_index("gx")
+    cells = index_ref.shape[1]
+    mine = pl.ds(pl.multiple_of(block * cells, LANES), cells)
+    moves = ((offset_hbm, offset), (length_hbm, length))
+    moves += ((index_hbm.at[:, mine], index_ref), (weight_hbm.at[:, mine], weight_ref))
+    heads = [
+        pltpu.make_async_copy(source, target, sems.at[number])
+        for number, (source, target) in enumerate(moves)
+    ]
+    for copy in heads:
+        copy.start()
+    for copy in heads:
+        copy.wait()
+    start, live = offset[block], length[block]
     rows = lax.broadcasted_iota(jnp.int32, (8, LANES), 0)
     taps = index_ref.shape[0]
     copies = []
-    for pair in range(matrix.shape[0]):
+    half_pairs = near_ref.shape[0]
+    for number in range(2 * half_pairs):
+        pair = (number + half_pairs) % (2 * half_pairs)
+        matrix, place = (near_ref, pair) if pair < half_pairs else (far_ref, pair - half_pairs)
         for side in range(2):
             lanes = slice((2 * pair + side) * LANES, (2 * pair + side + 1) * LANES)
             index = index_ref[:, lanes]
-            weight = jnp.where(index < length, weight_ref[:, lanes], 0.0)
+            weight = jnp.where(index < live, weight_ref[:, lanes], 0.0)
             inner = lax.rem(index + start, LANES)
             spots = [jnp.broadcast_to(inner[t : t + 1], (8, LANES)) for t in range(taps)]
             parts = []
@@ -146,7 +167,7 @@
                 part = jnp.where(index // LANES == m, weight, 0.0)
                 parts.append([jnp.broadcast_to(part[t : t + 1], (8, LANES)) for t in range(taps)])
 
-            def step(number, carry, side=side, pair=pair, spots=spots, parts=parts):
+            def step(number, carry, side=side, matrix=matrix, place=place, spots=spots, parts=parts):
                 near = [rows + 16 * number, rows + (16 * number + 8)]
                 hits = [[near[half] == spots[t] for t in range(taps)] for half in range(2)]
                 for m in range(SEGMENT):
@@ -158,14 +179,19 @@
                         total.append(terms[0])
                     high, low = halves(jnp.concatenate(total, 0))
                     at = pl.ds(pl.multiple_of(LANES * m + 16 * number, 16), 16)
-                    matrix[pair, 0, at, side * LANES : (side + 1) * LANES] = high
-                    matrix[pair, 1, at, side * LANES : (side + 1) * LANES] = low
+                    matrix[place, 0, at, side * LANES : (side + 1) * LANES] = high
+                    matrix[place, 1, at, side * LANES : (side + 1) * LANES] = low
                 return carry
 
             lax.fori_loop(0, LANES // 16, step, 0)
-        copies.append(pltpu.make_async_copy(matrix.at[pair], matrix_ref.at[pair], sems.at[pair]))
-        copies[-1].start()
-    return copies
+        if pair >= half_pairs:
+            copy = pltpu.make_async_copy(
+                far_ref.at[place], far_hbm.at[place], out_sems.at[place]
+            )
+            copies.append(copy)
+            copy.start()
+    for copy in copies:
+        copy.wait()
 
 
 def transform_kernel(
@@ -213,35 +239,11 @@
             out_ref[block, y, WINDOW - 1 :, :] = edges_ref[y : y + 1]
 
 
-def local_kernel(
-    z_low_ref, z_high_ref, y_low_ref, y_high_ref,
-    theta_hbm, sum_hbm, offset_hbm, length_hbm, index_hbm, weight_hbm, after_ref,
-    out_ref, matrix_ref,
-    theta, sums, offset, length, index, weight, matrix, sems, out_sems,
+def stencil_kernel(
+    z_low_ref, z_high_ref, y_low_ref, y_high_ref, theta_ref, sum_ref, after_ref,
+    local_hbm,
+    local_ref, sems,
 ):
-    block = lax.axis_index("gx")
-    cells = theta.shape[2]
-    mine = pl.ds(pl.multiple_of(block * cells, LANES), cells)
-    moves = ((offset_hbm, offset), (length_hbm, length))
-    moves += ((index_hbm.at[:, mine], index), (weight_hbm.at[:, mine], weight))
-    moves += ((theta_hbm, theta), (sum_hbm, sums))
-    copies = [
-        pltpu.make_async_copy(source, target, sems.at[number])
-        for number, (source, target) in enumerate(moves)
-    ]
-    for copy in copies:
-        copy.start()
-    for copy in copies[:4]:
-        copy.wait()
-    tails = fill_matrix(offset[block], length[block], index, weight, matrix, matrix_ref, out_sems)
-    for copy in copies[4:]:
-        copy.wait()
-    stencil(theta, sums, z_low_ref, z_high_ref, y_low_ref, y_high_ref, out_ref)
-    for copy in tails:
-        copy.wait()
-
-
-def stencil(theta_ref, sum_ref, z_low_ref, z_high_ref, y_low_ref, y_high_ref, out_ref):
     cells = theta_ref.shape[2]
     lane = lax.broadcasted_iota(jnp.int32, (8, cells), 1)
     planes = [ref[:, z, :] for ref in (z_low_ref, theta_ref, z_high_ref) for z in range(4)]
@@ -266,21 +268,26 @@
             laplace = laplace + second_coeffs[reach - 1] * (
                 (ahead_x + behind_x) + (ahead_y + behind_y) + (ahead_z + behind_z)
             )
-        out_ref[0, z] = grad_x
-        out_ref[1, z] = grad_y
-        out_ref[2, z] = grad_z
-        out_ref[3, z] = section_keep * sum_ref[:, z, :] + (time_step * diffusivity) * laplace
-        out_ref[4, z] = here
+        local_ref[0, z] = grad_x
+        local_ref[1, z] = grad_y
+        local_ref[2, z] = grad_z
+        local_ref[3, z] = section_keep * sum_ref[:, z, :] + (time_step * diffusivity) * laplace
+        local_ref[4, z] = here
+    copy = pltpu.make_async_copy(local_ref, local_hbm, sems.at[0])
+    copy.start()
+    copy.wait()
 
 
 def combine_kernel(
-    got_ref, matrix_hbm, local_ref, theta_ref, section_ref, matrix_ref, sems
+    got_ref, near_ref, far_hbm, local_hbm, theta_ref, section_ref, far_ref, local_ref, sems
 ):
+    half_pairs = near_ref.shape[0]
     copies = [
-        pltpu.make_async_copy(matrix_hbm.at[pair], matrix_ref.at[pair], sems.at[pair])
-        for pair in range(matrix_ref.shape[0])
-    ]
-    for copy in copies:
+        pltpu.make_async_copy(far_hbm.at[pair], far_ref.at[pair], sems.at[pair])
+        for pair in range(half_pairs)
+    ]
+    copies.append(pltpu.make_async_copy(local_hbm, local_ref, sems.at[half_pairs]))
+    for copy in copies[::-1]:
         copy.start()
     block = lax.axis_index("gx")
     blocks = got_ref.shape[0] // (12 * WINDOW)
@@ -308,9 +315,14 @@
     width = 2 * LANES
     for tile in range(cells // width):
         lanes = slice(tile * width, (tile + 1) * width)
-        copies[tile].wait()
-        twice = dot(both, matrix_ref[tile, 0])
-        carried = twice[:count] + twice[count:] + dot(high, matrix_ref[tile, 1])
+        matrix, pair = near_ref, tile
+        if tile >= half_pairs:
+            matrix, pair = far_ref, tile - half_pairs
+            copies[pair].wait()
+        twice = dot(both, matrix[pair, 0])
+        carried = twice[:count] + twice[count:] + dot(high, matrix[pair, 1])
+        if tile == 0:
+            copies[half_pairs].wait()
         for z in range(4):
             grad_x = local_ref[0, z, :, lanes]
             base = local_ref[3, z, :, lanes]
@@ -415,35 +427,36 @@
     (pieces,) = run(
         transform_kernel,
         "transform",
-        [VMEM] * 6 + [ANY] * 4,
+        [VMEM] * 6 + [ANY] * 2,
         [(f32(blocks, 12, WINDOW, LANES), VMEM)],
-    )(
-        columns.reshape(depth * 24, LANES), first, twiddle, left, turn, edges,
-        z_low, z_high, y_low, y_high,
-    )
+    )(columns.reshape(depth * 24, LANES), first, twiddle, left, turn, edges, z_low, z_high)
     arrived = lax.all_to_all(pieces, "gx", split_axis=0, concat_axis=0, tiled=True)
-    matrix_shape = (cells // (2 * LANES), 2, SEGMENT * LANES, 2 * LANES)
-    local, matrix = run(
-        local_kernel,
-        "local",
-        [VMEM] * 4 + [HBM] * 6 + [ANY],
-        [(f32(5, layers, rows_count, cells), VMEM), (pltpu.HBM(matrix_shape, jnp.bfloat16), HBM)],
-        [vmem(theta.shape, jnp.float32), vmem(theta.shape, jnp.float32)]
-        + [smem((blocks,), jnp.int32), smem((blocks,), jnp.int32)]
+    half_pairs = cells // (4 * LANES)
+    half = (half_pairs, 2, SEGMENT * LANES, 2 * LANES)
+    near, far = run(
+        matrix_kernel,
+        "matrix",
+        [HBM] * 4 + [ANY],
+        [(bf16(*half), VMEM), (pltpu.HBM(half, jnp.bfloat16), HBM)],
+        [smem((blocks,), jnp.int32), smem((blocks,), jnp.int32)]
         + [vmem((taps, cells), jnp.int32), vmem((taps, cells), jnp.float32)]
-        + [vmem(matrix_shape, jnp.bfloat16), dma((6,)), dma((matrix_shape[0],))],
-    )(
-        z_low, z_high, y_low, y_high,
-        theta, section_sum, seg_offset, seg_length, stencil_index, stencil_weight, pieces,
-    )
-    matrix = in_hbm(matrix)
+        + [vmem(half, jnp.bfloat16), dma((4,)), dma((half_pairs,))],
+    )(seg_offset, seg_length, stencil_index, stencil_weight, pieces)
+    local_shape = (5, layers, rows_count, cells)
+    (local,) = run(
+        stencil_kernel,
+        "stencil",
+        [VMEM] * 6 + [ANY],
+        [(pltpu.HBM(local_shape, jnp.float32), HBM)],
+        [vmem(local_shape, jnp.float32), dma((1,))],
+    )(z_low, z_high, y_low, y_high, theta, section_sum, pieces)
     return run(
         combine_kernel,
         "combine",
-        [VMEM, HBM, VMEM],
+        [VMEM, VMEM, HBM, HBM],
         [(f32(*theta.shape), VMEM), (f32(*theta.shape), VMEM)],
-        [vmem(matrix_shape, jnp.bfloat16), dma((matrix_shape[0],))],
-    )(arrived.reshape(blocks * 12 * WINDOW, LANES), matrix, local)
+        [vmem(half, jnp.bfloat16), vmem(local_shape, jnp.float32), dma((half_pairs + 1,))],
+    )(arrived.reshape(blocks * 12 * WINDOW, LANES), near, in_hbm(far), in_hbm(local))
 
 
 def solution(mesh):

time: 60.1 us -> 57.8 us (0.962)
  the two profiles are of different devices: /device:TPU:17 before, /device:TPU:16 now
where the time goes in v2:
time: 57.8 us; the launch traced here: 57.3 us
  starting transfers between devices  37.7 us (65%)
  Pallas kernels  13 us (22%)
  waiting for transfers between devices  5.78 us (10%)
  between operations  0.84 us (1%)
    all_to_all x1, starting transfers between devices, body(): lax.all_to_all(packed, 'gz', split_axis=0, concat_axis=0, tiled=True)  18.9 us
    ppermute x2, starting transfers between devices, neighbours(): lax.ppermute(edge_low, axis, [(b, a) for a, b in up])  7.76 us
    ppermute x2, starting transfers between devices, neighbours(): lax.ppermute(edge_high, axis, up)  5.75 us
    all_to_all x1, starting transfers between devices, body(): lax.all_to_all(pieces, 'gx', split_axis=0, concat_axis=0, tiled=True)  5.31 us
    pallas_call x1, Pallas kernels, body(): run(matrix_kernel, 'matrix', [HBM] * 4 + [ANY], [(bf16(*half), VMEM), (pl...  4.11 us
    all_to_all x1, waiting for transfers between devices, body(): lax.all_to_all(packed, 'gz', split_axis=0, concat_axis=0, tiled=True)  3.58 us
    pallas_call x1, Pallas kernels, body(): run(combine_kernel, 'combine', [VMEM, VMEM, HBM, HBM], [(f32(*theta.shape...  3.36 us
    all_to_all x1, waiting for transfers between devices, body(): lax.all_to_all(pieces, 'gx', split_axis=0, concat_axis=0, tiled=True)  2.18 us
  transfers between devices with their start and end apart: 6, of which 2 were waited for; matrix products, arithmetic and copies ran while one was open for 0% of the time, Pallas kernels for 14%

profile of v2, /device:TPU:16, one launch (start us, length us, event | category | flops | bytes accessed | tf_op | source)
XLA Modules:
  0.0 57.3 jit_solution(17499287614270968202)
XLA Ops:
  0.6 0.0 copy-start.2
  0.6 0.0 copy-start.4
  0.6 0.0 copy-start.6
  0.7 0.0 copy-start.7
  0.7 0.0 copy-start.8
  0.7 1.7 %pack.1 = (f32[16,24,128]{2,1,0:T(8,128)}, f32[4,4,1024]{2,1,0:T(4,128)S(1)}, f32[4,4,1024]{2,1,0:T(4,128)S(1)}) custom-call(f32[6,64,128]{2,1,0:T(8,128)} %bitcast.5, f32[8,4,1024]{2,1,0:T(4,128)} %theta_ref.3), custom_call_target="tpu_custom_call" | custom-call | flops 4000000000 | bytes 4000000 | tf_op jit(solution)/shard_map/pack/pallas_call | solution.py:403
  2.4 18.9 %all-to-all-start = ((f32[16,24,128]{2,1,0:T(8,128)}), f32[16,24,128]{2,1,0:T(8,128)S(1)}, u32[]{:S(2)}, u32[]{:S(2)}) async-start(f32[16,24,128]{2,1,0:T(8,128)} %get-tuple-element.12), calls=%async_computation | async-start | bytes 393216 | tf_op jit(solution)/shard_map/all_to_all | solution.py:410
  21.3 0.0 copy-done.2
  21.3 3.8 %collective-permute-start = (f32[8,4,1024]{2,1,0:T(4,128)S(1)}, f32[8,4,1024]{2,1,0:T(4,128)S(1)}, u32[]{:S(2)}, u32[]{:S(2)}) collective-permute-start(f32[8,4,1024]{2,1,0:T(4,128)S(1)} %copy-done.2), channel_id=1, source_target_pairs={{0,1},{1,2},{2,3},{3,4},{4,5},{5,6},{6,7},{7,8},{8,9},{9,10},{10,1... | collective-permute-start | bytes 393224 | tf_op jit(solution)/shard_map/ppermute | solution.py:392
  25.1 3.2 %collective-permute-start.1 = (f32[8,4,1024]{2,1,0:T(4,128)S(1)}, f32[8,4,1024]{2,1,0:T(4,128)S(1)}, u32[]{:S(2)}, u32[]{:S(2)}) collective-permute-start(f32[8,4,1024]{2,1,0:T(4,128)S(1)} %copy-done.2), channel_id=1, source_target_pairs={{1,0},{2,1},{3,2},{4,3},{5,4},{6,5},{7,6},{8,7},{9,8},{10,9},{11,1... | collective-permute-start | bytes 393224 | tf_op jit(solution)/shard_map/ppermute | solution.py:392
  28.4 1.9 %collective-permute-start.2 = (f32[4,4,1024]{2,1,0:T(4,128)S(1)}, f32[4,4,1024]{2,1,0:T(4,128)S(1)}, u32[]{:S(2)}, u32[]{:S(2)}) collective-permute-start(f32[4,4,1024]{2,1,0:T(4,128)S(1)} %get-tuple-element.20), channel_id=1, source_target_pairs={{0,16},{16,32},{32,48},{48,64},{64,80},{80,96},{96,112},{112,0},{1... | collective-permute-start | bytes 196616 | tf_op jit(solution)/shard_map/ppermute | solution.py:392
  30.3 4.5 %collective-permute-start.3 = (f32[4,4,1024]{2,1,0:T(4,128)S(1)}, f32[4,4,1024]{2,1,0:T(4,128)S(1)}, u32[]{:S(2)}, u32[]{:S(2)}) collective-permute-start(f32[4,4,1024]{2,1,0:T(4,128)S(1)} %get-tuple-element.21), channel_id=1, source_target_pairs={{16,0},{32,16},{48,32},{64,48},{80,64},{96,80},{112,96},{0,112},{1... | collective-permute-start | bytes 196616 | tf_op jit(solution)/shard_map/ppermute | solution.py:392
  34.9 0.0 copy-done.4
  34.9 0.0 copy-done.6
  34.9 0.0 copy-done.7
  34.9 0.0 copy-done.8
  34.9 0.7 %setup.1 = (bf16[64,192]{1,0:T(8,128)(2,1)S(1)}, f32[8,128]{1,0:T(8,128)S(1)}, f32[8,128]{1,0:T(8,128)S(1)}, bf16[384,256]{1,0:T(8,128)(2,1)S(1)}, f32[2,32,128]{2,1,0:T(8,128)S(1)}) custom-call(s32[8]{0:T(128)S(1)} %copy-done.4, f32[8,4,1024]{2,1,0:T(4,128)S(1)} %copy-done.2, f32[32,8,192]{2,1,0:T(8,128)S(1)} %copy-done.6, bf16[384,256]{1,0:T(8,128)(2,1)S(1)} %copy-done.7, ...), custom_call_target="tpu_custom_call" | custom-call | flops 4000000000 | bytes 4000000 | tf_op jit(solution)/shard_map/setup/pallas_call | solution.py:413
  35.6 0.0 collective-permute-done.after_and_out_0_.z_low_ref
  35.6 0.0 collective-permute-done.1.after_and_out_1_.z_high_ref
  35.6 3.6 %all-to-all-done = f32[16,24,128]{2,1,0:T(8,128)S(1)} async-done(((f32[16,24,128]{2,1,0:T(8,128)}), f32[16,24,128]{2,1,0:T(8,128)S(1)}, u32[]{:S(2)}, u32[]{:S(2)}) %all-to-all-start) | async-done | bytes 196640 | tf_op jit(solution)/shard_map/all_to_all | solution.py:410
  39.2 1.5 %transform.1.after_ref = f32[8,12,8,128]{3,2,1,0:T(8,128)} custom-call(f32[384,128]{1,0:T(8,128)S(1)} %bitcast.4, bf16[384,256]{1,0:T(8,128)(2,1)S(1)} %get-tuple-element.13.first_ref, f32[2,32,128]{2,1,0:T(8,128)S(1)} %get-tuple-element.14.twiddle_ref, bf16[64,192]{1,0:T(8,128)(2,1)S(1)} %get-tuple-element.15.left_ref, ...), custom_call_target="tpu_custom_call" | custom-call | flops 4000000000 | bytes 4000000 | tf_op jit(solution)/shard_map/transform/pallas_call | solution.py:427
  40.7 5.3 %all-to-all-start.1 = ((f32[8,12,8,128]{3,2,1,0:T(8,128)}), f32[8,12,8,128]{3,2,1,0:T(8,128)S(1)}, u32[]{:S(2)}, u32[]{:S(2)}) async-start(f32[8,12,8,128]{3,2,1,0:T(8,128)} %transform.1.after_ref), calls=%async_computation.1 | async-start | bytes 786432 | tf_op jit(solution)/shard_map/all_to_all | solution.py:433
  46.0 0.0 copy-done
  46.0 0.0 copy-done.1
  46.0 0.0 copy-done.5
  46.0 0.0 copy-start.3
  46.0 4.1 %matrix.1 = (bf16[2,2,768,256]{3,2,1,0:T(8,128)(2,1)S(1)}, bf16[2,2,768,256]{3,2,1,0:T(8,128)(2,1)}) custom-call(s32[8]{0:T(128)S(1)} %copy-done.4, s32[8]{0:T(128)S(1)} %copy-done.5, s32[8,8192]{1,0:T(8,128)S(1)} %copy-done, f32[8,8192]{1,0:T(8,128)S(1)} %copy-done.1, f32[8,12,8,128]{3,2,1,0:T(8,128)} %transform.1.after_ref), custom_call_target="tpu_custom_call" | custom-call | flops 4000000000 | bytes 4000000 | tf_op jit(solution)/shard_map/matrix/pallas_call | solution.py:436
  50.2 0.0 collective-permute-done.2.y_low_ref
  50.2 0.0 collective-permute-done.3.y_high_ref
  50.2 1.6 %stencil.1.local_hbm = f32[5,4,8,1024]{3,2,1,0:T(8,128)} custom-call(f32[8,4,1024]{2,1,0:T(4,128)S(1)} %collective-permute-done.after_and_out_0_.z_low_ref, f32[8,4,1024]{2,1,0:T(4,128)S(1)} %collective-permute-done.1.after_and_out_1_.z_high_ref, f32[4,4,1024]{2,1,0:T(4,128)S(1)} %collective-permute-done.2.y_low_ref, ...), custom_call_target="tpu_custom_call" | custom-call | flops 4000000000 | bytes 4000000 | tf_op jit(solution)/shard_map/stencil/pallas_call | solution.py:446
  51.8 2.2 %all-to-all-done.1 = f32[8,12,8,128]{3,2,1,0:T(8,128)S(1)} async-done(((f32[8,12,8,128]{3,2,1,0:T(8,128)}), f32[8,12,8,128]{3,2,1,0:T(8,128)S(1)}, u32[]{:S(2)}, u32[]{:S(2)}) %all-to-all-start.1) | async-done | bytes 393248 | tf_op jit(solution)/shard_map/all_to_all | solution.py:433
  54.0 3.4 %combine.1 = (f32[8,4,1024]{2,1,0:T(4,128)}, f32[8,4,1024]{2,1,0:T(4,128)}) custom-call(f32[768,128]{1,0:T(8,128)S(1)} %bitcast.3, bf16[2,2,768,256]{3,2,1,0:T(8,128)(2,1)S(1)} %get-tuple-element.18.near_ref, bf16[2,2,768,256]{3,2,1,0:T(8,128)(2,1)} %get-tuple-element.19.far_hbm, f32[5,4,8,1024]{3,2,1,0:T(8,128)} %stencil.1.local_hbm), custom_call_target="tpu_custom_call" | custom-call | flops 4000000000 | bytes 4000000 | tf_op jit(solution)/shard_map/combine/pallas_call | solution.py:453
  (4 shorter events, 0.0 us)
Async XLA Ops:
  0.6 20.7 %copy-start.2 = (f32[8,4,1024]{2,1,0:T(4,128)S(1)}, f32[8,4,1024]{2,1,0:T(4,128)}, u32[]{:S(2)}) copy-start(f32[8,4,1024]{2,1,0:T(4,128)} %theta_ref.3) | copy-start | bytes 393220
  0.6 34.2 %copy-start.4 = (s32[8]{0:T(128)S(1)}, s32[8]{0:T(128)}, u32[]{:S(2)}) copy-start(s32[8]{0:T(128)} %offset_hbm.3) | copy-start | bytes 100
  0.6 34.2 %copy-start.6 = (f32[32,8,192]{2,1,0:T(8,128)S(1)}, f32[32,8,192]{2,1,0:T(8,128)}, u32[]{:S(2)}) copy-start(f32[32,8,192]{2,1,0:T(8,128)} %constant.8.clone.last_hbm) | copy-start | bytes 589828
  0.7 34.2 %copy-start.7 = (bf16[384,256]{1,0:T(8,128)(2,1)S(1)}, bf16[384,256]{1,0:T(8,128)(2,1)}, u32[]{:S(2)}) copy-start(bf16[384,256]{1,0:T(8,128)(2,1)} %constant.6.clone.first_hbm) | copy-start | bytes 589828
  0.7 34.2 %copy-start.8 = (f32[2,32,128]{2,1,0:T(8,128)S(1)}, f32[2,32,128]{2,1,0:T(8,128)}, u32[]{:S(2)}) copy-start(f32[2,32,128]{2,1,0:T(8,128)} %constant.7.clone.twiddle_hbm) | copy-start | bytes 98308
  2.4 36.8 %all-to-all-start = ((f32[16,24,128]{2,1,0:T(8,128)}), f32[16,24,128]{2,1,0:T(8,128)S(1)}, u32[]{:S(2)}, u32[]{:S(2)}) async-start(f32[16,24,128]{2,1,0:T(8,128)} %get-tuple-element.12), calls=%async_computation | async-start | bytes 393216 | tf_op jit(solution)/shard_map/all_to_all | solution.py:410
  21.3 14.3 %collective-permute-start = (f32[8,4,1024]{2,1,0:T(4,128)S(1)}, f32[8,4,1024]{2,1,0:T(4,128)S(1)}, u32[]{:S(2)}, u32[]{:S(2)}) collective-permute-start(f32[8,4,1024]{2,1,0:T(4,128)S(1)} %copy-done.2), channel_id=1, source_target_pairs={{0,1},{1,2},{2,3},{3,4},{4,5},{5,6},{6,7},{7,8},{8,9},{9,10},{10,1... | collective-permute-start | bytes 393224 | tf_op jit(solution)/shard_map/ppermute | solution.py:392
  25.1 10.5 %collective-permute-start.1 = (f32[8,4,1024]{2,1,0:T(4,128)S(1)}, f32[8,4,1024]{2,1,0:T(4,128)S(1)}, u32[]{:S(2)}, u32[]{:S(2)}) collective-permute-start(f32[8,4,1024]{2,1,0:T(4,128)S(1)} %copy-done.2), channel_id=1, source_target_pairs={{1,0},{2,1},{3,2},{4,3},{5,4},{6,5},{7,6},{8,7},{9,8},{10,9},{11,1... | collective-permute-start | bytes 393224 | tf_op jit(solution)/shard_map/ppermute | solution.py:392
  28.4 21.8 %collective-permute-start.2 = (f32[4,4,1024]{2,1,0:T(4,128)S(1)}, f32[4,4,1024]{2,1,0:T(4,128)S(1)}, u32[]{:S(2)}, u32[]{:S(2)}) collective-permute-start(f32[4,4,1024]{2,1,0:T(4,128)S(1)} %get-tuple-element.20), channel_id=1, source_target_pairs={{0,16},{16,32},{32,48},{48,64},{64,80},{80,96},{96,112},{112,0},{1... | collective-permute-start | bytes 196616 | tf_op jit(solution)/shard_map/ppermute | solution.py:392
  30.3 19.9 %collective-permute-start.3 = (f32[4,4,1024]{2,1,0:T(4,128)S(1)}, f32[4,4,1024]{2,1,0:T(4,128)S(1)}, u32[]{:S(2)}, u32[]{:S(2)}) collective-permute-start(f32[4,4,1024]{2,1,0:T(4,128)S(1)} %get-tuple-element.21), channel_id=1, source_target_pairs={{16,0},{32,16},{48,32},{64,48},{80,64},{96,80},{112,96},{0,112},{1... | collective-permute-start | bytes 196616 | tf_op jit(solution)/shard_map/ppermute | solution.py:392
  39.2 6.8 %copy-start = (s32[8,8192]{1,0:T(8,128)S(1)}, s32[8,8192]{1,0:T(8,128)}, u32[]{:S(2)}) copy-start(s32[8,8192]{1,0:T(8,128)} %index_hbm.1) | copy-start | bytes 786436
  39.2 6.8 %copy-start.1 = (f32[8,8192]{1,0:T(8,128)S(1)}, f32[8,8192]{1,0:T(8,128)}, u32[]{:S(2)}) copy-start(f32[8,8192]{1,0:T(8,128)} %weight_hbm.1) | copy-start | bytes 786436
  39.2 6.8 %copy-start.5 = (s32[8]{0:T(128)S(1)}, s32[8]{0:T(128)}, u32[]{:S(2)}) copy-start(s32[8]{0:T(128)} %length_hbm.1) | copy-start | bytes 100
  40.7 13.3 %all-to-all-start.1 = ((f32[8,12,8,128]{3,2,1,0:T(8,128)}), f32[8,12,8,128]{3,2,1,0:T(8,128)S(1)}, u32[]{:S(2)}, u32[]{:S(2)}) async-start(f32[8,12,8,128]{3,2,1,0:T(8,128)} %transform.1.after_ref), calls=%async_computation.1 | async-start | bytes 786432 | tf_op jit(solution)/shard_map/all_to_all | solution.py:433
  46.0 4.1 %copy-start.3 = (f32[8,4,1024]{2,1,0:T(4,128)S(1)}, f32[8,4,1024]{2,1,0:T(4,128)}, u32[]{:S(2)}) copy-start(f32[8,4,1024]{2,1,0:T(4,128)} %sum_ref.1) | copy-start | bytes 393220

commit v3 on v2

--- a/solution.py
+++ b/solution.py
@@ -20,6 +20,8 @@
 LANES = 128
 LOW = 32
 SEGMENT = 6
+PAIRS = 4
+NEAR = 2
 WINDOW = 8
 VMEM_LIMIT = 16 * 1024 * 1024
 
@@ -60,7 +62,7 @@
 
 
 def pack_kernel(spectrum_ref, theta_ref, out_ref, low_ref, high_ref, got, packed, sems):
-    groups, dests, rows = 2, out_ref.shape[0], theta_ref.shape[0]
+    groups, dests, rows = 4, out_ref.shape[0], theta_ref.shape[0]
     count = dests // groups
     heads = [
         pltpu.make_async_copy(
@@ -108,8 +110,8 @@
 
 def setup_kernel(
     offset_hbm, theta_hbm, last_hbm, first_hbm, twiddle_hbm,
-    left_ref, turn_ref, edges_ref, first_ref, twiddle_ref,
-    offset, theta, last, sems,
+    left_ref, turn_ref, edges_ref, first_ref, twiddle_ref, theta,
+    offset, last, sems,
 ):
     moves = ((offset_hbm, offset), (theta_hbm, theta), (last_hbm, last))
     moves += ((first_hbm, first_ref), (twiddle_hbm, twiddle_ref))
@@ -131,18 +133,19 @@
 
 
 def matrix_kernel(
-    offset_hbm, length_hbm, index_hbm, weight_hbm, after_ref,
-    near_ref, far_hbm,
-    offset, length, index_ref, weight_ref, far_ref, sems, out_sems,
+    near, offset_hbm, length_hbm, index_ref, weight_ref, after_ref, *outs_and_scratch
 ):
+    count = PAIRS
+    refs, far_hbms = outs_and_scratch[:near], outs_and_scratch[near:count]
+    offset, length = outs_and_scratch[count : count + 2]
+    refs = refs + outs_and_scratch[count + 2 : -2]
+    sems, out_sems = outs_and_scratch[-2:]
     block = lax.axis_index("gx")
-    cells = index_ref.shape[1]
-    mine = pl.ds(pl.multiple_of(block * cells, LANES), cells)
-    moves = ((offset_hbm, offset), (length_hbm, length))
-    moves += ((index_hbm.at[:, mine], index_ref), (weight_hbm.at[:, mine], weight_ref))
+    cells = index_ref.shape[1] // lax.axis_size("gx")
+    first_cell = block * cells
     heads = [
         pltpu.make_async_copy(source, target, sems.at[number])
-        for number, (source, target) in enumerate(moves)
+        for number, (source, target) in enumerate(((offset_hbm, offset), (length_hbm, length)))
     ]
     for copy in heads:
         copy.start()
@@ -152,12 +155,11 @@
     rows = lax.broadcasted_iota(jnp.int32, (8, LANES), 0)
     taps = index_ref.shape[0]
     copies = []
-    half_pairs = near_ref.shape[0]
-    for number in range(2 * half_pairs):
-        pair = (number + half_pairs) % (2 * half_pairs)
-        matrix, place = (near_ref, pair) if pair < half_pairs else (far_ref, pair - half_pairs)
+    for number in range(PAIRS):
+        pair = (number + near) % PAIRS
+        matrix = refs[pair]
         for side in range(2):
-            lanes = slice((2 * pair + side) * LANES, (2 * pair + side + 1) * LANES)
+            lanes = pl.ds(pl.multiple_of(first_cell + (2 * pair + side) * LANES, LANES), LANES)
             index = index_ref[:, lanes]
             weight = jnp.where(index < live, weight_ref[:, lanes], 0.0)
             inner = lax.rem(index + start, LANES)
@@ -167,29 +169,29 @@
                 part = jnp.where(index // LANES == m, weight, 0.0)
                 parts.append([jnp.broadcast_to(part[t : t + 1], (8, LANES)) for t in range(taps)])
 
-            def step(number, carry, side=side, matrix=matrix, place=place, spots=spots, parts=parts):
-                near = [rows + 16 * number, rows + (16 * number + 8)]
-                hits = [[near[half] == spots[t] for t in range(taps)] for half in range(2)]
+            def step(number, carry, side=side, matrix=matrix, spots=spots, parts=parts):
+                sums = []
+                for half in range(2):
+                    near = rows + (16 * number + 8 * half)
+                    hits = [near == spots[t] for t in range(taps)]
+                    for m in range(SEGMENT):
+                        total = jnp.where(hits[0], parts[m][0], 0.0)
+                        for t in range(1, taps):
+                            total = jnp.where(hits[t], total + parts[m][t], total)
+                        sums.append(total)
                 for m in range(SEGMENT):
-                    total = []
-                    for half in range(2):
-                        terms = [jnp.where(hits[half][t], parts[m][t], 0.0) for t in range(taps)]
-                        while len(terms) > 1:
-                            terms = [a + b for a, b in zip(terms[::2], terms[1::2], strict=True)]
-                        total.append(terms[0])
-                    high, low = halves(jnp.concatenate(total, 0))
+                    high, low = halves(jnp.concatenate([sums[m], sums[SEGMENT + m]], 0))
                     at = pl.ds(pl.multiple_of(LANES * m + 16 * number, 16), 16)
-                    matrix[place, 0, at, side * LANES : (side + 1) * LANES] = high
-                    matrix[place, 1, at, side * LANES : (side + 1) * LANES] = low
+                    matrix[0, at, side * LANES : (side + 1) * LANES] = high
+                    matrix[1, at, side * LANES : (side + 1) * LANES] = low
                 return carry
 
             lax.fori_loop(0, LANES // 16, step, 0)
-        if pair >= half_pairs:
-            copy = pltpu.make_async_copy(
-                far_ref.at[place], far_hbm.at[place], out_sems.at[place]
+        if pair >= near:
+            copies.append(
+                pltpu.make_async_copy(matrix, far_hbms[pair - near], out_sems.at[pair - near])
             )
-            copies.append(copy)
-            copy.start()
+            copies[-1].start()
     for copy in copies:
         copy.wait()
 
@@ -278,16 +280,16 @@
     copy.wait()
 
 
-def combine_kernel(
-    got_ref, near_ref, far_hbm, local_hbm, theta_ref, section_ref, far_ref, local_ref, sems
-):
-    half_pairs = near_ref.shape[0]
+def combine_kernel(near, got_ref, local_hbm, *refs):
+    matrices, far_hbms = refs[:near] + refs[PAIRS + 2 : -2], refs[near:PAIRS]
+    theta_ref, section_ref = refs[PAIRS : PAIRS + 2]
+    local_ref, sems = refs[-2:]
+    moves = list(zip(far_hbms, matrices[near:], strict=True)) + [(local_hbm, local_ref)]
     copies = [
-        pltpu.make_async_copy(far_hbm.at[pair], far_ref.at[pair], sems.at[pair])
-        for pair in range(half_pairs)
-    ]
-    copies.append(pltpu.make_async_copy(local_hbm, local_ref, sems.at[half_pairs]))
-    for copy in copies[::-1]:
+        pltpu.make_async_copy(source, target, sems.at[number])
+        for number, (source, target) in enumerate(moves)
+    ]
+    for copy in copies:
         copy.start()
     block = lax.axis_index("gx")
     blocks = got_ref.shape[0] // (12 * WINDOW)
@@ -313,16 +315,16 @@
     after = halo_of(lax.rem(block + 1, blocks))
     lane = lax.broadcasted_iota(jnp.int32, (8, LANES), 1)
     width = 2 * LANES
+    carried_of = []
+    for tile in range(cells // width):
+        if tile >= near:
+            copies[tile - near].wait()
+        twice = dot(both, matrices[tile][0])
+        carried_of.append(twice[:count] + twice[count:] + dot(high, matrices[tile][1]))
+    copies[-1].wait()
     for tile in range(cells // width):
         lanes = slice(tile * width, (tile + 1) * width)
-        matrix, pair = near_ref, tile
-        if tile >= half_pairs:
-            matrix, pair = far_ref, tile - half_pairs
-            copies[pair].wait()
-        twice = dot(both, matrix[pair, 0])
-        carried = twice[:count] + twice[count:] + dot(high, matrix[pair, 1])
-        if tile == 0:
-            copies[half_pairs].wait()
+        carried = carried_of[tile]
         for z in range(4):
             grad_x = local_ref[0, z, :, lanes]
             base = local_ref[3, z, :, lanes]
@@ -395,7 +397,6 @@
 def body(spectrum, theta, section_sum, seg_offset, seg_length, stencil_index, stencil_weight):
     blocks, depth = lax.axis_size("gx"), lax.axis_size("gz")
     rows_count, layers, cells = theta.shape
-    taps = stencil_index.shape[0]
     first, twiddle, last = (jnp.asarray(t) for t in tables())
     vmem, smem, dma = pltpu.VMEM, pltpu.SMEM, pltpu.SemaphoreType.DMA
 
@@ -405,12 +406,11 @@
         "pack",
         [HBM, HBM],
         [(f32(depth, 24, LANES), HBM), (edge, HBM), (edge, HBM)],
-        [vmem((6, 4 * depth, LANES), jnp.float32), vmem((depth, 24, LANES), jnp.float32), dma((6,))],
+        [vmem((6, 4 * depth, LANES), jnp.float32), vmem((depth, 24, LANES), jnp.float32), dma((10,))],
     )(in_hbm(spectrum.reshape(6, 4 * depth, LANES)), in_hbm(theta))
     columns = lax.all_to_all(packed, "gz", split_axis=0, concat_axis=0, tiled=True)
-    z_low, z_high = neighbours(theta, theta, "gz")
     y_low, y_high = neighbours(y_first, y_last, "gy")
-    left, turn, edges, first, twiddle = run(
+    left, turn, edges, first, twiddle, copied = run(
         setup_kernel,
         "setup",
         [HBM] * 5,
@@ -420,28 +420,31 @@
             (f32(8, LANES), VMEM),
             (bf16(*first.shape), VMEM),
             (f32(*twiddle.shape), VMEM),
+            (f32(*theta.shape), VMEM),
         ],
-        [smem((blocks,), jnp.int32), vmem(theta.shape, jnp.float32), vmem(last.shape, jnp.float32)]
+        [smem((blocks,), jnp.int32), vmem(last.shape, jnp.float32)]
         + [dma((5,))],
     )(seg_offset, theta, last, first, twiddle)
+    z_low, z_high = neighbours(copied, copied, "gz")
     (pieces,) = run(
         transform_kernel,
         "transform",
-        [VMEM] * 6 + [ANY] * 2,
+        [VMEM] * 6,
         [(f32(blocks, 12, WINDOW, LANES), VMEM)],
-    )(columns.reshape(depth * 24, LANES), first, twiddle, left, turn, edges, z_low, z_high)
+    )(columns.reshape(depth * 24, LANES), first, twiddle, left, turn, edges)
     arrived = lax.all_to_all(pieces, "gx", split_axis=0, concat_axis=0, tiled=True)
-    half_pairs = cells // (4 * LANES)
-    half = (half_pairs, 2, SEGMENT * LANES, 2 * LANES)
-    near, far = run(
-        matrix_kernel,
+    part = (2, SEGMENT * LANES, cells // PAIRS)
+    far_parts = [vmem(part, jnp.bfloat16)] * (PAIRS - NEAR)
+    matrices = run(
+        functools.partial(matrix_kernel, NEAR),
         "matrix",
-        [HBM] * 4 + [ANY],
-        [(bf16(*half), VMEM), (pltpu.HBM(half, jnp.bfloat16), HBM)],
+        [HBM, HBM, VMEM, VMEM, ANY],
+        [(bf16(*part), VMEM)] * NEAR + [(pltpu.HBM(part, jnp.bfloat16), HBM)] * (PAIRS - NEAR),
         [smem((blocks,), jnp.int32), smem((blocks,), jnp.int32)]
-        + [vmem((taps, cells), jnp.int32), vmem((taps, cells), jnp.float32)]
-        + [vmem(half, jnp.bfloat16), dma((4,)), dma((half_pairs,))],
+        + far_parts
+        + [dma((2,)), dma((PAIRS,))],
     )(seg_offset, seg_length, stencil_index, stencil_weight, pieces)
+    matrices = matrices[:NEAR] + tuple(in_hbm(far) for far in matrices[NEAR:])
     local_shape = (5, layers, rows_count, cells)
     (local,) = run(
         stencil_kernel,
@@ -451,12 +454,12 @@
         [vmem(local_shape, jnp.float32), dma((1,))],
     )(z_low, z_high, y_low, y_high, theta, section_sum, pieces)
     return run(
-        combine_kernel,
+        functools.partial(combine_kernel, NEAR),
         "combine",
-        [VMEM, VMEM, HBM, HBM],
+        [VMEM, HBM] + [VMEM] * NEAR + [HBM] * (PAIRS - NEAR),
         [(f32(*theta.shape), VMEM), (f32(*theta.shape), VMEM)],
-        [vmem(half, jnp.bfloat16), vmem(local_shape, jnp.float32), dma((half_pairs + 1,))],
-    )(arrived.reshape(blocks * 12 * WINDOW, LANES), near, in_hbm(far), in_hbm(local))
+        far_parts + [vmem(local_shape, jnp.float32), dma((PAIRS + 1,))],
+    )(arrived.reshape(blocks * 12 * WINDOW, LANES), in_hbm(local), *matrices)
 
 
 def solution(mesh):

time: 57.8 us -> 56.5 us (0.978)
  waiting for transfers between devices: 5.78 us -> 4.74 us
    ppermute x2, starting transfers between devices: 5.75 us -> 3.84 us  [neighbours(): lax.ppermute(edge_high, axis, up)]
    ppermute x2, starting transfers between devices: 7.76 us -> 9.59 us  [neighbours(): lax.ppermute(edge_low, axis, [(b, a) for a, b in up])]
    all_to_all x1, waiting for transfers between devices: 3.58 us -> 2.38 us  [body(): lax.all_to_all(packed, 'gz', split_axis=0, concat_axis=0, tiled=True)]
where the time goes in v3:
time: 56.5 us; the launch traced here: 56.1 us
  starting transfers between devices  37.9 us (67%)
  Pallas kernels  12.5 us (22%)
  waiting for transfers between devices  4.74 us (8%)
  between operations  0.85 us (2%)
    all_to_all x1, starting transfers between devices, body(): lax.all_to_all(packed, 'gz', split_axis=0, concat_axis=0, tiled=True)  19 us
    ppermute x2, starting transfers between devices, neighbours(): lax.ppermute(edge_low, axis, [(b, a) for a, b in up])  9.59 us
    all_to_all x1, starting transfers between devices, body(): lax.all_to_all(pieces, 'gx', split_axis=0, concat_axis=0, tiled=True)  5.44 us
    pallas_call x1, Pallas kernels, body(): run(functools.partial(matrix_kernel, NEAR), 'matrix', [HBM, HBM, VMEM, VM...  3.91 us
    ppermute x2, starting transfers between devices, neighbours(): lax.ppermute(edge_high, axis, up)  3.84 us
    pallas_call x1, Pallas kernels, body(): run(functools.partial(combine_kernel, NEAR), 'combine', [VMEM, HBM] + [VM...  3.21 us
    all_to_all x1, waiting for transfers between devices, body(): lax.all_to_all(packed, 'gz', split_axis=0, concat_axis=0, tiled=True)  2.38 us
    all_to_all x1, waiting for transfers between devices, body(): lax.all_to_all(pieces, 'gx', split_axis=0, concat_axis=0, tiled=True)  2.35 us
  transfers between devices with their start and end apart: 6, of which 2 were waited for; matrix products, arithmetic and copies ran while one was open for 0% of the time, Pallas kernels for 14%

profile of v3, /device:TPU:16, one launch (start us, length us, event | category | flops | bytes accessed | tf_op | source)
XLA Modules:
  0.0 56.1 jit_solution(3434681467669051423)
XLA Ops:
  0.6 0.0 copy-start.7
  0.6 0.0 copy-start.8
  0.7 1.6 %pack.1 = (f32[16,24,128]{2,1,0:T(8,128)}, f32[4,4,1024]{2,1,0:T(4,128)S(1)}, f32[4,4,1024]{2,1,0:T(4,128)S(1)}) custom-call(f32[6,64,128]{2,1,0:T(8,128)} %bitcast.5, f32[8,4,1024]{2,1,0:T(4,128)} %theta_ref.3), custom_call_target="tpu_custom_call" | custom-call | flops 4000000000 | bytes 4000000 | tf_op jit(solution)/shard_map/pack/pallas_call | solution.py:404
  2.3 0.0 copy-start.6
  2.3 0.0 copy-start.2
  2.3 0.0 copy-start.4
  2.3 19.0 %all-to-all-start = ((f32[16,24,128]{2,1,0:T(8,128)}), f32[16,24,128]{2,1,0:T(8,128)S(1)}, u32[]{:S(2)}, u32[]{:S(2)}) async-start(f32[16,24,128]{2,1,0:T(8,128)} %get-tuple-element.15), calls=%async_computation | async-start | bytes 393216 | tf_op jit(solution)/shard_map/all_to_all | solution.py:411
  21.3 0.0 copy-done.7
  21.3 0.0 copy-done.8
  21.4 0.0 copy-done.6
  21.4 0.0 copy-done.2
  21.4 0.0 copy-done.4
  21.4 0.7 %setup.1 = (bf16[64,192]{1,0:T(8,128)(2,1)S(1)}, f32[8,128]{1,0:T(8,128)S(1)}, f32[8,128]{1,0:T(8,128)S(1)}, bf16[384,256]{1,0:T(8,128)(2,1)S(1)}, f32[2,32,128]{2,1,0:T(8,128)S(1)}, /*index=5*/f32[8,4,1024]{2,1,0:T(4,128)S(1)}) custom-call(s32[8]{0:T(128)S(1)} %copy-done.4, f32[8,4,1024]{2,1,0:T(4,128)S(1)} %copy-done.2, f32[32,8,192]{2,1,0:T(8,128)S(1)} %copy-done.6, ...), custom_call_target="tpu_custom_call" | custom-call | flops 4000000000 | bytes 4000000 | tf_op jit(solution)/shard_map/setup/pallas_call | solution.py:413
  22.1 5.0 %collective-permute-start.1 = (f32[8,4,1024]{2,1,0:T(4,128)S(1)}, f32[8,4,1024]{2,1,0:T(4,128)S(1)}, u32[]{:S(2)}, u32[]{:S(2)}) collective-permute-start(f32[8,4,1024]{2,1,0:T(4,128)S(1)} %get-tuple-element.21), channel_id=1, source_target_pairs={{1,0},{2,1},{3,2},{4,3},{5,4},{6,5},{7,6},{8,7},{9,8},{10,9},{11,1... | collective-permute-start | bytes 393224 | tf_op jit(solution)/shard_map/ppermute | solution.py:394
  27.1 1.9 %collective-permute-start = (f32[8,4,1024]{2,1,0:T(4,128)S(1)}, f32[8,4,1024]{2,1,0:T(4,128)S(1)}, u32[]{:S(2)}, u32[]{:S(2)}) collective-permute-start(f32[8,4,1024]{2,1,0:T(4,128)S(1)} %get-tuple-element.21), channel_id=1, source_target_pairs={{0,1},{1,2},{2,3},{3,4},{4,5},{5,6},{6,7},{7,8},{8,9},{9,10},{10,1... | collective-permute-start | bytes 393224 | tf_op jit(solution)/shard_map/ppermute | solution.py:394
  29.1 1.9 %collective-permute-start.2 = (f32[4,4,1024]{2,1,0:T(4,128)S(1)}, f32[4,4,1024]{2,1,0:T(4,128)S(1)}, u32[]{:S(2)}, u32[]{:S(2)}) collective-permute-start(f32[4,4,1024]{2,1,0:T(4,128)S(1)} %get-tuple-element.22), channel_id=1, source_target_pairs={{0,16},{16,32},{32,48},{48,64},{64,80},{80,96},{96,112},{112,0},{1... | collective-permute-start | bytes 196616 | tf_op jit(solution)/shard_map/ppermute | solution.py:394
  31.0 4.5 %collective-permute-start.3 = (f32[4,4,1024]{2,1,0:T(4,128)S(1)}, f32[4,4,1024]{2,1,0:T(4,128)S(1)}, u32[]{:S(2)}, u32[]{:S(2)}) collective-permute-start(f32[4,4,1024]{2,1,0:T(4,128)S(1)} %get-tuple-element.23), channel_id=1, source_target_pairs={{16,0},{32,16},{48,32},{64,48},{80,64},{96,80},{112,96},{0,112},{1... | collective-permute-start | bytes 196616 | tf_op jit(solution)/shard_map/ppermute | solution.py:394
  35.5 2.4 %all-to-all-done = f32[16,24,128]{2,1,0:T(8,128)S(1)} async-done(((f32[16,24,128]{2,1,0:T(8,128)}), f32[16,24,128]{2,1,0:T(8,128)S(1)}, u32[]{:S(2)}, u32[]{:S(2)}) %all-to-all-start) | async-done | bytes 196640 | tf_op jit(solution)/shard_map/all_to_all | solution.py:411
  37.9 1.5 %transform.1.after_ref = f32[8,12,8,128]{3,2,1,0:T(8,128)} custom-call(f32[384,128]{1,0:T(8,128)S(1)} %bitcast.4, bf16[384,256]{1,0:T(8,128)(2,1)S(1)} %get-tuple-element.16.first_ref, f32[2,32,128]{2,1,0:T(8,128)S(1)} %get-tuple-element.17.twiddle_ref, bf16[64,192]{1,0:T(8,128)(2,1)S(1)} %get-tuple-element.18.left_ref, ...), custom_call_target="tpu_custom_call" | custom-call | flops 4000000000 | bytes 4000000 | tf_op jit(solution)/shard_map/transform/pallas_call | solution.py:429
  39.4 5.4 %all-to-all-start.1 = ((f32[8,12,8,128]{3,2,1,0:T(8,128)}), f32[8,12,8,128]{3,2,1,0:T(8,128)S(1)}, u32[]{:S(2)}, u32[]{:S(2)}) async-start(f32[8,12,8,128]{3,2,1,0:T(8,128)} %transform.1.after_ref), calls=%async_computation.1 | async-start | bytes 786432 | tf_op jit(solution)/shard_map/all_to_all | solution.py:435
  44.9 0.0 copy-done
  44.9 0.0 copy-done.1
  44.9 0.0 copy-done.5
  44.9 0.0 copy-start.3
  44.9 3.9 %matrix.1 = (bf16[2,768,256]{2,1,0:T(8,128)(2,1)S(1)}, bf16[2,768,256]{2,1,0:T(8,128)(2,1)S(1)}, bf16[2,768,256]{2,1,0:T(8,128)(2,1)}, bf16[2,768,256]{2,1,0:T(8,128)(2,1)}) custom-call(s32[8]{0:T(128)S(1)} %copy-done.4, s32[8]{0:T(128)S(1)} %copy-done.5, s32[8,8192]{1,0:T(8,128)S(1)} %copy-done, f32[8,8192]{1,0:T(8,128)S(1)} %copy-done.1, ...), custom_call_target="tpu_custom_call" | custom-call | flops 4000000000 | bytes 4000000 | tf_op jit(solution)/shard_map/matrix/pallas_call | solution.py:438
  48.8 0.0 collective-permute-done.2.y_low_ref
  48.8 0.0 collective-permute-done.3.y_high_ref
  48.8 0.0 collective-permute-done.1.z_high_ref
  48.9 0.0 collective-permute-done.z_low_ref
  48.9 1.6 %stencil.1.local_hbm = f32[5,4,8,1024]{3,2,1,0:T(8,128)} custom-call(f32[8,4,1024]{2,1,0:T(4,128)S(1)} %collective-permute-done.z_low_ref, f32[8,4,1024]{2,1,0:T(4,128)S(1)} %collective-permute-done.1.z_high_ref, f32[4,4,1024]{2,1,0:T(4,128)S(1)} %collective-permute-done.2.y_low_ref, f32[4,4,1024]{2,1,0:T(4,128)S(1)} %collective-permute-done.3.y_high_ref, ...), custom_call_target="tpu_custom_call" | custom-call | flops 4000000000 | bytes 4000000 | tf_op jit(solution)/shard_map/stencil/pallas_call | solution.py:449
  50.5 2.4 %all-to-all-done.1 = f32[8,12,8,128]{3,2,1,0:T(8,128)S(1)} async-done(((f32[8,12,8,128]{3,2,1,0:T(8,128)}), f32[8,12,8,128]{3,2,1,0:T(8,128)S(1)}, u32[]{:S(2)}, u32[]{:S(2)}) %all-to-all-start.1) | async-done | bytes 393248 | tf_op jit(solution)/shard_map/all_to_all | solution.py:435
  52.9 3.2 %combine.1 = (f32[8,4,1024]{2,1,0:T(4,128)}, f32[8,4,1024]{2,1,0:T(4,128)}) custom-call(f32[768,128]{1,0:T(8,128)S(1)} %bitcast.3, f32[5,4,8,1024]{3,2,1,0:T(8,128)} %stencil.1.local_hbm, bf16[2,768,256]{2,1,0:T(8,128)(2,1)S(1)} %get-tuple-element.24.refs_0_, bf16[2,768,256]{2,1,0:T(8,128)(2,1)S(1)} %get-tuple-element.25.refs_1_, ...), custom_call_target="tpu_custom_call" | custom-call | flops 4000000000 | bytes 4000000 | tf_op jit(solution)/shard_map/combine/pallas_call | solution.py:456
  (4 shorter events, 0.0 us)
Async XLA Ops:
  0.6 20.7 %copy-start.7 = (bf16[384,256]{1,0:T(8,128)(2,1)S(1)}, bf16[384,256]{1,0:T(8,128)(2,1)}, u32[]{:S(2)}) copy-start(bf16[384,256]{1,0:T(8,128)(2,1)} %constant.6.clone.first_hbm) | copy-start | bytes 589828
  0.6 20.7 %copy-start.8 = (f32[2,32,128]{2,1,0:T(8,128)S(1)}, f32[2,32,128]{2,1,0:T(8,128)}, u32[]{:S(2)}) copy-start(f32[2,32,128]{2,1,0:T(8,128)} %constant.7.clone.twiddle_hbm) | copy-start | bytes 98308
  2.3 19.1 %copy-start.6 = (f32[32,8,192]{2,1,0:T(8,128)S(1)}, f32[32,8,192]{2,1,0:T(8,128)}, u32[]{:S(2)}) copy-start(f32[32,8,192]{2,1,0:T(8,128)} %constant.8.clone.last_hbm) | copy-start | bytes 589828
  2.3 19.1 %copy-start.2 = (f32[8,4,1024]{2,1,0:T(4,128)S(1)}, f32[8,4,1024]{2,1,0:T(4,128)}, u32[]{:S(2)}) copy-start(f32[8,4,1024]{2,1,0:T(4,128)} %theta_ref.3) | copy-start | bytes 393220
  2.3 19.1 %copy-start.4 = (s32[8]{0:T(128)S(1)}, s32[8]{0:T(128)}, u32[]{:S(2)}) copy-start(s32[8]{0:T(128)} %offset_hbm.3) | copy-start | bytes 100
  2.3 35.6 %all-to-all-start = ((f32[16,24,128]{2,1,0:T(8,128)}), f32[16,24,128]{2,1,0:T(8,128)S(1)}, u32[]{:S(2)}, u32[]{:S(2)}) async-start(f32[16,24,128]{2,1,0:T(8,128)} %get-tuple-element.15), calls=%async_computation | async-start | bytes 393216 | tf_op jit(solution)/shard_map/all_to_all | solution.py:411
  22.1 26.8 %collective-permute-start.1 = (f32[8,4,1024]{2,1,0:T(4,128)S(1)}, f32[8,4,1024]{2,1,0:T(4,128)S(1)}, u32[]{:S(2)}, u32[]{:S(2)}) collective-permute-start(f32[8,4,1024]{2,1,0:T(4,128)S(1)} %get-tuple-element.21), channel_id=1, source_target_pairs={{1,0},{2,1},{3,2},{4,3},{5,4},{6,5},{7,6},{8,7},{9,8},{10,9},{11,1... | collective-permute-start | bytes 393224 | tf_op jit(solution)/shard_map/ppermute | solution.py:394
  27.1 21.7 %collective-permute-start = (f32[8,4,1024]{2,1,0:T(4,128)S(1)}, f32[8,4,1024]{2,1,0:T(4,128)S(1)}, u32[]{:S(2)}, u32[]{:S(2)}) collective-permute-start(f32[8,4,1024]{2,1,0:T(4,128)S(1)} %get-tuple-element.21), channel_id=1, source_target_pairs={{0,1},{1,2},{2,3},{3,4},{4,5},{5,6},{6,7},{7,8},{8,9},{9,10},{10,1... | collective-permute-start | bytes 393224 | tf_op jit(solution)/shard_map/ppermute | solution.py:394
  29.1 19.8 %collective-permute-start.2 = (f32[4,4,1024]{2,1,0:T(4,128)S(1)}, f32[4,4,1024]{2,1,0:T(4,128)S(1)}, u32[]{:S(2)}, u32[]{:S(2)}) collective-permute-start(f32[4,4,1024]{2,1,0:T(4,128)S(1)} %get-tuple-element.22), channel_id=1, source_target_pairs={{0,16},{16,32},{32,48},{48,64},{64,80},{80,96},{96,112},{112,0},{1... | collective-permute-start | bytes 196616 | tf_op jit(solution)/shard_map/ppermute | solution.py:394
  31.0 17.8 %collective-permute-start.3 = (f32[4,4,1024]{2,1,0:T(4,128)S(1)}, f32[4,4,1024]{2,1,0:T(4,128)S(1)}, u32[]{:S(2)}, u32[]{:S(2)}) collective-permute-start(f32[4,4,1024]{2,1,0:T(4,128)S(1)} %get-tuple-element.23), channel_id=1, source_target_pairs={{16,0},{32,16},{48,32},{64,48},{80,64},{96,80},{112,96},{0,112},{1... | collective-permute-start | bytes 196616 | tf_op jit(solution)/shard_map/ppermute | solution.py:394
  39.4 5.5 %copy-start = (s32[8,8192]{1,0:T(8,128)S(1)}, s32[8,8192]{1,0:T(8,128)}, u32[]{:S(2)}) copy-start(s32[8,8192]{1,0:T(8,128)} %index_ref.1) | copy-start | bytes 786436
  39.4 5.5 %copy-start.1 = (f32[8,8192]{1,0:T(8,128)S(1)}, f32[8,8192]{1,0:T(8,128)}, u32[]{:S(2)}) copy-start(f32[8,8192]{1,0:T(8,128)} %weight_ref.1) | copy-start | bytes 786436
  39.4 5.5 %copy-start.5 = (s32[8]{0:T(128)S(1)}, s32[8]{0:T(128)}, u32[]{:S(2)}) copy-start(s32[8]{0:T(128)} %length_hbm.1) | copy-start | bytes 100
  39.4 13.4 %all-to-all-start.1 = ((f32[8,12,8,128]{3,2,1,0:T(8,128)}), f32[8,12,8,128]{3,2,1,0:T(8,128)S(1)}, u32[]{:S(2)}, u32[]{:S(2)}) async-start(f32[8,12,8,128]{3,2,1,0:T(8,128)} %transform.1.after_ref), calls=%async_computation.1 | async-start | bytes 786432 | tf_op jit(solution)/shard_map/all_to_all | solution.py:435
  44.9 4.0 %copy-start.3 = (f32[8,4,1024]{2,1,0:T(4,128)S(1)}, f32[8,4,1024]{2,1,0:T(4,128)}, u32[]{:S(2)}) copy-start(f32[8,4,1024]{2,1,0:T(4,128)} %sum_ref.1) | copy-start | bytes 393220

commit v4 on v3

--- a/solution.py
+++ b/solution.py
@@ -61,8 +61,8 @@
     return np.concatenate([first_high, first_high, first_low], 0), twiddle, last_all
 
 
-def pack_kernel(spectrum_ref, theta_ref, out_ref, low_ref, high_ref, got, packed, sems):
-    groups, dests, rows = 4, out_ref.shape[0], theta_ref.shape[0]
+def pack_kernel(spectrum_ref, out_ref, got, packed, sems):
+    groups, dests = 4, out_ref.shape[0]
     count = dests // groups
     heads = [
         pltpu.make_async_copy(
@@ -80,11 +80,7 @@
         )
         for group in range(groups)
     ]
-    sides = [
-        pltpu.make_async_copy(theta_ref.at[pl.ds(0, 4)], low_ref, sems.at[2 * groups]),
-        pltpu.make_async_copy(theta_ref.at[pl.ds(rows - 4, 4)], high_ref, sems.at[2 * groups + 1]),
-    ]
-    for copy in heads + sides:
+    for copy in heads:
         copy.start()
     for group in range(groups):
         heads[group].wait()
@@ -92,7 +88,7 @@
             for part in range(6):
                 packed[dest, 4 * part : 4 * part + 4, :] = got[part, 4 * dest : 4 * dest + 4, :]
         tails[group].start()
-    for copy in tails + sides:
+    for copy in tails:
         copy.wait()
 
 
@@ -109,27 +105,25 @@
 
 
 def setup_kernel(
-    offset_hbm, theta_hbm, last_hbm, first_hbm, twiddle_hbm,
-    left_ref, turn_ref, edges_ref, first_ref, twiddle_ref, theta,
-    offset, last, sems,
+    offset_hbm, theta_in, last, first_in, twiddle_in,
+    left_ref, turn_ref, edges_ref, first_ref, twiddle_ref, theta, y_first_ref, y_last_ref,
+    offset, sems,
 ):
-    moves = ((offset_hbm, offset), (theta_hbm, theta), (last_hbm, last))
-    moves += ((first_hbm, first_ref), (twiddle_hbm, twiddle_ref))
-    copies = [
-        pltpu.make_async_copy(source, target, sems.at[number])
-        for number, (source, target) in enumerate(moves)
-    ]
-    for copy in copies:
-        copy.start()
-    for copy in copies:
-        copy.wait()
+    copy = pltpu.make_async_copy(offset_hbm, offset, sems.at[0])
+    copy.start()
+    theta[...] = theta_in[...]
+    y_first_ref[...] = theta_in[:4]
+    y_last_ref[...] = theta_in[theta_in.shape[0] - 4 :]
+    first_ref[...] = first_in[...]
+    twiddle_ref[...] = twiddle_in[...]
+    edges_ref[...] = edges_of(theta_in)
+    copy.wait()
     blocks = left_ref.shape[0] // WINDOW
     left = [last[offset[block] // LANES] for block in range(blocks)]
     left_ref[...] = jnp.concatenate(left, 0).astype(jnp.bfloat16)
     lane = lax.broadcasted_iota(jnp.int32, (1, LANES), 1)
     for block in range(blocks):
         turn_ref[block : block + 1, :] = jnp.where(lane < offset[block] % LANES, 1.0, 0.0)
-    edges_ref[...] = edges_of(theta)
 
 
 def matrix_kernel(
@@ -401,19 +395,18 @@
     vmem, smem, dma = pltpu.VMEM, pltpu.SMEM, pltpu.SemaphoreType.DMA
 
     edge = f32(4, layers, cells)
-    packed, y_first, y_last = run(
+    (packed,) = run(
         pack_kernel,
         "pack",
-        [HBM, HBM],
-        [(f32(depth, 24, LANES), HBM), (edge, HBM), (edge, HBM)],
-        [vmem((6, 4 * depth, LANES), jnp.float32), vmem((depth, 24, LANES), jnp.float32), dma((10,))],
-    )(in_hbm(spectrum.reshape(6, 4 * depth, LANES)), in_hbm(theta))
+        [HBM],
+        [(f32(depth, 24, LANES), HBM)],
+        [vmem((6, 4 * depth, LANES), jnp.float32), vmem((depth, 24, LANES), jnp.float32), dma((8,))],
+    )(in_hbm(spectrum.reshape(6, 4 * depth, LANES)))
     columns = lax.all_to_all(packed, "gz", split_axis=0, concat_axis=0, tiled=True)
-    y_low, y_high = neighbours(y_first, y_last, "gy")
-    left, turn, edges, first, twiddle, copied = run(
+    left, turn, edges, first, twiddle, copied, y_first, y_last = run(
         setup_kernel,
         "setup",
-        [HBM] * 5,
+        [HBM] + [VMEM] * 4,
         [
             (bf16(blocks * WINDOW, last.shape[2]), VMEM),
             (f32(blocks, LANES), VMEM),
@@ -421,10 +414,12 @@
             (bf16(*first.shape), VMEM),
             (f32(*twiddle.shape), VMEM),
             (f32(*theta.shape), VMEM),
+            (edge, VMEM),
+            (edge, VMEM),
         ],
-        [smem((blocks,), jnp.int32), vmem(last.shape, jnp.float32)]
-        + [dma((5,))],
+        [smem((blocks,), jnp.int32), dma((1,))],
     )(seg_offset, theta, last, first, twiddle)
+    y_low, y_high = neighbours(y_first, y_last, "gy")
     z_low, z_high = neighbours(copied, copied, "gz")
     (pieces,) = run(
         transform_kernel,

time: 56.5 us -> 56.5 us (level)
  no operation moved by 1% of the time
where the time goes in v4:
time: 56.5 us; the launch traced here: 56.1 us
  starting transfers between devices  37.9 us (67%)
  Pallas kernels  12.5 us (22%)
  waiting for transfers between devices  4.81 us (9%)
  between operations  0.85 us (2%)
    all_to_all x1, starting transfers between devices, body(): lax.all_to_all(packed, 'gz', split_axis=0, concat_axis=0, tiled=True)  19 us
    ppermute x2, starting transfers between devices, neighbours(): lax.ppermute(edge_low, axis, [(b, a) for a, b in up])  9.59 us
    all_to_all x1, starting transfers between devices, body(): lax.all_to_all(pieces, 'gx', split_axis=0, concat_axis=0, tiled=True)  5.45 us
    pallas_call x1, Pallas kernels, body(): run(functools.partial(matrix_kernel, NEAR), 'matrix', [HBM, HBM, VMEM, VM...  3.91 us
    ppermute x2, starting transfers between devices, neighbours(): lax.ppermute(edge_high, axis, up)  3.84 us
    pallas_call x1, Pallas kernels, body(): run(functools.partial(combine_kernel, NEAR), 'combine', [VMEM, HBM] + [VM...  3.21 us
    all_to_all x1, waiting for transfers between devices, body(): lax.all_to_all(packed, 'gz', split_axis=0, concat_axis=0, tiled=True)  2.45 us
    all_to_all x1, waiting for transfers between devices, body(): lax.all_to_all(pieces, 'gx', split_axis=0, concat_axis=0, tiled=True)  2.35 us
  transfers between devices with their start and end apart: 6, of which 2 were waited for; matrix products, arithmetic and copies ran while one was open for 0% of the time, Pallas kernels for 14%

profile of v4, /device:TPU:16, one launch (start us, length us, event | category | flops | bytes accessed | tf_op | source)
XLA Modules:
  0.0 56.1 jit_solution(5107381024872784869)
XLA Ops:
  0.6 0.0 copy-start.6
  0.6 1.6 %pack.1 = f32[16,24,128]{2,1,0:T(8,128)} custom-call(f32[6,64,128]{2,1,0:T(8,128)} %bitcast.5), custom_call_target="tpu_custom_call" | custom-call | flops 4000000000 | bytes 4000000 | tf_op jit(solution)/shard_map/pack/pallas_call | solution.py:398
  2.3 0.0 copy-start.2
  2.3 0.0 copy-start.4
  2.3 0.0 copy-start.7
  2.3 0.0 copy-start.8
  2.3 19.0 %all-to-all-start = ((f32[16,24,128]{2,1,0:T(8,128)}), f32[16,24,128]{2,1,0:T(8,128)S(1)}, u32[]{:S(2)}, u32[]{:S(2)}) async-start(f32[16,24,128]{2,1,0:T(8,128)} %pack.1), calls=%async_computation | async-start | bytes 393216 | tf_op jit(solution)/shard_map/all_to_all | solution.py:405
  21.3 0.0 copy-done.6
  21.3 0.0 copy-done.2
  21.3 0.0 copy-done.4
  21.4 0.0 copy-done.7
  21.4 0.0 copy-done.8
  21.4 0.6 %setup.1 = (bf16[64,192]{1,0:T(8,128)(2,1)S(1)}, f32[8,128]{1,0:T(8,128)S(1)}, f32[8,128]{1,0:T(8,128)S(1)}, bf16[384,256]{1,0:T(8,128)(2,1)S(1)}, f32[2,32,128]...) custom-call(s32[8]{0:T(128)S(1)} %copy-done.4, ...), custom_call_target="tpu_custom_call" | custom-call | flops 4000000000 | bytes 4000000 | tf_op jit(solution)/shard_map/setup/pallas_call | solution.py:406
  22.0 5.0 %collective-permute-start.1 = (f32[8,4,1024]{2,1,0:T(4,128)S(1)}, f32[8,4,1024]{2,1,0:T(4,128)S(1)}, u32[]{:S(2)}, u32[]{:S(2)}) collective-permute-start(f32[8,4,1024]{2,1,0:T(4,128)S(1)} %get-tuple-element.19), channel_id=1, source_target_pairs={{1,0},{2,1},{3,2},{4,3},{5,4},{6,5},{7,6},{8,7},{9,8},{10,9},{11,1... | collective-permute-start | bytes 393224 | tf_op jit(solution)/shard_map/ppermute | solution.py:388
  27.1 1.9 %collective-permute-start = (f32[8,4,1024]{2,1,0:T(4,128)S(1)}, f32[8,4,1024]{2,1,0:T(4,128)S(1)}, u32[]{:S(2)}, u32[]{:S(2)}) collective-permute-start(f32[8,4,1024]{2,1,0:T(4,128)S(1)} %get-tuple-element.19), channel_id=1, source_target_pairs={{0,1},{1,2},{2,3},{3,4},{4,5},{5,6},{6,7},{7,8},{8,9},{9,10},{10,1... | collective-permute-start | bytes 393224 | tf_op jit(solution)/shard_map/ppermute | solution.py:388
  29.0 1.9 %collective-permute-start.2 = (f32[4,4,1024]{2,1,0:T(4,128)S(1)}, f32[4,4,1024]{2,1,0:T(4,128)S(1)}, u32[]{:S(2)}, u32[]{:S(2)}) collective-permute-start(f32[4,4,1024]{2,1,0:T(4,128)S(1)} %get-tuple-element.20), channel_id=1, source_target_pairs={{0,16},{16,32},{32,48},{48,64},{64,80},{80,96},{96,112},{112,0},{1... | collective-permute-start | bytes 196616 | tf_op jit(solution)/shard_map/ppermute | solution.py:388
  30.9 4.5 %collective-permute-start.3 = (f32[4,4,1024]{2,1,0:T(4,128)S(1)}, f32[4,4,1024]{2,1,0:T(4,128)S(1)}, u32[]{:S(2)}, u32[]{:S(2)}) collective-permute-start(f32[4,4,1024]{2,1,0:T(4,128)S(1)} %get-tuple-element.21), channel_id=1, source_target_pairs={{16,0},{32,16},{48,32},{64,48},{80,64},{96,80},{112,96},{0,112},{1... | collective-permute-start | bytes 196616 | tf_op jit(solution)/shard_map/ppermute | solution.py:388
  35.5 2.5 %all-to-all-done = f32[16,24,128]{2,1,0:T(8,128)S(1)} async-done(((f32[16,24,128]{2,1,0:T(8,128)}), f32[16,24,128]{2,1,0:T(8,128)S(1)}, u32[]{:S(2)}, u32[]{:S(2)}) %all-to-all-start) | async-done | bytes 196640 | tf_op jit(solution)/shard_map/all_to_all | solution.py:405
  37.9 1.5 %transform.1.after_ref = f32[8,12,8,128]{3,2,1,0:T(8,128)} custom-call(f32[384,128]{1,0:T(8,128)S(1)} %bitcast.4, bf16[384,256]{1,0:T(8,128)(2,1)S(1)} %get-tuple-element.14.first_ref, f32[2,32,128]{2,1,0:T(8,128)S(1)} %get-tuple-element.15.twiddle_ref, bf16[64,192]{1,0:T(8,128)(2,1)S(1)} %get-tuple-element.16.left_ref, ...), custom_call_target="tpu_custom_call" | custom-call | flops 4000000000 | bytes 4000000 | tf_op jit(solution)/shard_map/transform/pallas_call | solution.py:424
  39.4 5.4 %all-to-all-start.1 = ((f32[8,12,8,128]{3,2,1,0:T(8,128)}), f32[8,12,8,128]{3,2,1,0:T(8,128)S(1)}, u32[]{:S(2)}, u32[]{:S(2)}) async-start(f32[8,12,8,128]{3,2,1,0:T(8,128)} %transform.1.after_ref), calls=%async_computation.1 | async-start | bytes 786432 | tf_op jit(solution)/shard_map/all_to_all | solution.py:430
  44.9 0.0 copy-done
  44.9 0.0 copy-done.1
  44.9 0.0 copy-done.5
  44.9 0.0 copy-start.3
  44.9 3.9 %matrix.1 = (bf16[2,768,256]{2,1,0:T(8,128)(2,1)S(1)}, bf16[2,768,256]{2,1,0:T(8,128)(2,1)S(1)}, bf16[2,768,256]{2,1,0:T(8,128)(2,1)}, bf16[2,768,256]{2,1,0:T(8,128)(2,1)}) custom-call(s32[8]{0:T(128)S(1)} %copy-done.4, s32[8]{0:T(128)S(1)} %copy-done.5, s32[8,8192]{1,0:T(8,128)S(1)} %copy-done, f32[8,8192]{1,0:T(8,128)S(1)} %copy-done.1, ...), custom_call_target="tpu_custom_call" | custom-call | flops 4000000000 | bytes 4000000 | tf_op jit(solution)/shard_map/matrix/pallas_call | solution.py:433
  48.8 0.0 collective-permute-done.2.y_low_ref
  48.8 0.0 collective-permute-done.3.y_high_ref
  48.8 0.0 collective-permute-done.1.z_high_ref
  48.9 0.0 collective-permute-done.z_low_ref
  48.9 1.6 %stencil.1.local_hbm = f32[5,4,8,1024]{3,2,1,0:T(8,128)} custom-call(f32[8,4,1024]{2,1,0:T(4,128)S(1)} %collective-permute-done.z_low_ref, f32[8,4,1024]{2,1,0:T(4,128)S(1)} %collective-permute-done.1.z_high_ref, f32[4,4,1024]{2,1,0:T(4,128)S(1)} %collective-permute-done.2.y_low_ref, f32[4,4,1024]{2,1,0:T(4,128)S(1)} %collective-permute-done.3.y_high_ref, ...), custom_call_target="tpu_custom_call" | custom-call | flops 4000000000 | bytes 4000000 | tf_op jit(solution)/shard_map/stencil/pallas_call | solution.py:444
  50.5 2.3 %all-to-all-done.1 = f32[8,12,8,128]{3,2,1,0:T(8,128)S(1)} async-done(((f32[8,12,8,128]{3,2,1,0:T(8,128)}), f32[8,12,8,128]{3,2,1,0:T(8,128)S(1)}, u32[]{:S(2)}, u32[]{:S(2)}) %all-to-all-start.1) | async-done | bytes 393248 | tf_op jit(solution)/shard_map/all_to_all | solution.py:430
  52.9 3.2 %combine.1 = (f32[8,4,1024]{2,1,0:T(4,128)}, f32[8,4,1024]{2,1,0:T(4,128)}) custom-call(f32[768,128]{1,0:T(8,128)S(1)} %bitcast.3, f32[5,4,8,1024]{3,2,1,0:T(8,128)} %stencil.1.local_hbm, bf16[2,768,256]{2,1,0:T(8,128)(2,1)S(1)} %get-tuple-element.22.refs_0_, bf16[2,768,256]{2,1,0:T(8,128)(2,1)S(1)} %get-tuple-element.23.refs_1_, ...), custom_call_target="tpu_custom_call" | custom-call | flops 4000000000 | bytes 4000000 | tf_op jit(solution)/shard_map/combine/pallas_call | solution.py:451
  (4 shorter events, 0.0 us)
Async XLA Ops:
  0.6 20.7 %copy-start.6 = (f32[32,8,192]{2,1,0:T(8,128)S(1)}, f32[32,8,192]{2,1,0:T(8,128)}, u32[]{:S(2)}) copy-start(f32[32,8,192]{2,1,0:T(8,128)} %constant.8.clone.last) | copy-start | bytes 589828
  2.3 19.1 %copy-start.2 = (f32[8,4,1024]{2,1,0:T(4,128)S(1)}, f32[8,4,1024]{2,1,0:T(4,128)}, u32[]{:S(2)}) copy-start(f32[8,4,1024]{2,1,0:T(4,128)} %theta_ref.1) | copy-start | bytes 393220
  2.3 19.1 %copy-start.4 = (s32[8]{0:T(128)S(1)}, s32[8]{0:T(128)}, u32[]{:S(2)}) copy-start(s32[8]{0:T(128)} %offset_hbm.3) | copy-start | bytes 100
  2.3 19.1 %copy-start.7 = (bf16[384,256]{1,0:T(8,128)(2,1)S(1)}, bf16[384,256]{1,0:T(8,128)(2,1)}, u32[]{:S(2)}) copy-start(bf16[384,256]{1,0:T(8,128)(2,1)} %constant.6.clone.first_in) | copy-start | bytes 589828
  2.3 19.1 %copy-start.8 = (f32[2,32,128]{2,1,0:T(8,128)S(1)}, f32[2,32,128]{2,1,0:T(8,128)}, u32[]{:S(2)}) copy-start(f32[2,32,128]{2,1,0:T(8,128)} %constant.7.clone.twiddle_in) | copy-start | bytes 98308
  2.3 35.6 %all-to-all-start = ((f32[16,24,128]{2,1,0:T(8,128)}), f32[16,24,128]{2,1,0:T(8,128)S(1)}, u32[]{:S(2)}, u32[]{:S(2)}) async-start(f32[16,24,128]{2,1,0:T(8,128)} %pack.1), calls=%async_computation | async-start | bytes 393216 | tf_op jit(solution)/shard_map/all_to_all | solution.py:405
  22.0 26.8 %collective-permute-start.1 = (f32[8,4,1024]{2,1,0:T(4,128)S(1)}, f32[8,4,1024]{2,1,0:T(4,128)S(1)}, u32[]{:S(2)}, u32[]{:S(2)}) collective-permute-start(f32[8,4,1024]{2,1,0:T(4,128)S(1)} %get-tuple-element.19), channel_id=1, source_target_pairs={{1,0},{2,1},{3,2},{4,3},{5,4},{6,5},{7,6},{8,7},{9,8},{10,9},{11,1... | collective-permute-start | bytes 393224 | tf_op jit(solution)/shard_map/ppermute | solution.py:388
  27.1 21.8 %collective-permute-start = (f32[8,4,1024]{2,1,0:T(4,128)S(1)}, f32[8,4,1024]{2,1,0:T(4,128)S(1)}, u32[]{:S(2)}, u32[]{:S(2)}) collective-permute-start(f32[8,4,1024]{2,1,0:T(4,128)S(1)} %get-tuple-element.19), channel_id=1, source_target_pairs={{0,1},{1,2},{2,3},{3,4},{4,5},{5,6},{6,7},{7,8},{8,9},{9,10},{10,1... | collective-permute-start | bytes 393224 | tf_op jit(solution)/shard_map/ppermute | solution.py:388
  29.0 19.8 %collective-permute-start.2 = (f32[4,4,1024]{2,1,0:T(4,128)S(1)}, f32[4,4,1024]{2,1,0:T(4,128)S(1)}, u32[]{:S(2)}, u32[]{:S(2)}) collective-permute-start(f32[4,4,1024]{2,1,0:T(4,128)S(1)} %get-tuple-element.20), channel_id=1, source_target_pairs={{0,16},{16,32},{32,48},{48,64},{64,80},{80,96},{96,112},{112,0},{1... | collective-permute-start | bytes 196616 | tf_op jit(solution)/shard_map/ppermute | solution.py:388
  30.9 17.9 %collective-permute-start.3 = (f32[4,4,1024]{2,1,0:T(4,128)S(1)}, f32[4,4,1024]{2,1,0:T(4,128)S(1)}, u32[]{:S(2)}, u32[]{:S(2)}) collective-permute-start(f32[4,4,1024]{2,1,0:T(4,128)S(1)} %get-tuple-element.21), channel_id=1, source_target_pairs={{16,0},{32,16},{48,32},{64,48},{80,64},{96,80},{112,96},{0,112},{1... | collective-permute-start | bytes 196616 | tf_op jit(solution)/shard_map/ppermute | solution.py:388
  39.4 5.5 %copy-start = (s32[8,8192]{1,0:T(8,128)S(1)}, s32[8,8192]{1,0:T(8,128)}, u32[]{:S(2)}) copy-start(s32[8,8192]{1,0:T(8,128)} %index_ref.1) | copy-start | bytes 786436
  39.4 5.5 %copy-start.1 = (f32[8,8192]{1,0:T(8,128)S(1)}, f32[8,8192]{1,0:T(8,128)}, u32[]{:S(2)}) copy-start(f32[8,8192]{1,0:T(8,128)} %weight_ref.1) | copy-start | bytes 786436
  39.4 5.5 %copy-start.5 = (s32[8]{0:T(128)S(1)}, s32[8]{0:T(128)}, u32[]{:S(2)}) copy-start(s32[8]{0:T(128)} %length_hbm.1) | copy-start | bytes 100
  39.4 13.4 %all-to-all-start.1 = ((f32[8,12,8,128]{3,2,1,0:T(8,128)}), f32[8,12,8,128]{3,2,1,0:T(8,128)S(1)}, u32[]{:S(2)}, u32[]{:S(2)}) async-start(f32[8,12,8,128]{3,2,1,0:T(8,128)} %transform.1.after_ref), calls=%async_computation.1 | async-start | bytes 786432 | tf_op jit(solution)/shard_map/all_to_all | solution.py:430
  44.9 4.0 %copy-start.3 = (f32[8,4,1024]{2,1,0:T(4,128)S(1)}, f32[8,4,1024]{2,1,0:T(4,128)}, u32[]{:S(2)}) copy-start(f32[8,4,1024]{2,1,0:T(4,128)} %sum_ref.1) | copy-start | bytes 393220
